TPU v7x, 512 devices: a whole 4x8x8 slice. The times are simulated.
512 devices in a mesh: seq: 16 (over x, z_hi), head: 8 (over y), dp: 4 (over z_lo, core).
Axes of the slice: x: 4, y: 8, z: 8 (z_hi: 4, z_lo: 2; z = z_hi * 2 + z_lo), core: 2. Of those that a mesh axis runs over, the one named last changes fastest.
Arguments:
- queries: bfloat16 [32768, 4096], P(('dp', 'seq'), 'head'), parts along dimension 0, may hold values from -6 to 6
- key_vectors: bfloat16 [32768, 4096], P(('dp', 'seq'), 'head'), parts along dimension 0, may hold values from -6 to 6
- value_vectors: bfloat16 [32768, 4096], P(('dp', 'seq'), 'head'), parts along dimension 0, may hold values from -13 to 13
- norm_gain: float32 [4096], P('head'), may hold values from 0.1 to 1.9
- cotangent: bfloat16 [32768, 4096], P(('dp', 'seq'), 'head'), parts along dimension 0, may hold values from -6 to 6
Outputs:
- layer_out: bfloat16 [32768, 4096], P(('dp', 'seq'), 'head'), parts along dimension 0
- grad_query: bfloat16 [32768, 4096], P(('dp', 'seq'), 'head'), parts along dimension 0
- grad_key: bfloat16 [32768, 4096], P(('dp', 'seq'), 'head'), parts along dimension 0
- grad_value: bfloat16 [32768, 4096], P(('dp', 'seq'), 'head'), parts along dimension 0
There are 4 independent parts, one for each index of `dp`. A program takes and returns all parts, laid end to end along the dimension named above; an argument that names none is the same for every part. Nothing has to cross between parts.
All inputs are finite; a program needn't handle non-finite values.
Results may differ from a plain program's by a relative error of at most 0.0058.
Values sent between devices are 32-bit elements; how exact they have to be, the bound alone decides.
No kernel may reach another device: no remote copies, remote signals or barrier semaphores. Data moves between devices by JAX's collectives and lax.ppermute only.
A program may use at most 64 MiB of HBM per device.

v0:
```python
import jax
import jax.numpy as jnp
from jax import lax
from jax.sharding import PartitionSpec as P

HD = 128
FEAT = 4096


EPS = 1e-06


def from_behind(block, axis, distance):
    devices = range(lax.axis_size(axis))
    route = [(i - distance, i) for i in devices if i - distance in devices]
    return lax.ppermute(block, axis, route)


def forward_prefix(own_total):
    empty_state = jnp.zeros_like(own_total)

    def forward_relay_turn(turn_index, carried):
        moving, summed = carried
        moving = from_behind(moving, "seq", 1)
        return (moving, summed + moving)

    return lax.fori_loop(0, lax.axis_size("seq") - 1, forward_relay_turn, (own_total, empty_state))[
        1
    ]


def backward_suffix(own_total):
    empty_state = jnp.zeros_like(own_total)

    def backward_relay_turn(turn_index, carried):
        moving, summed = carried
        moving = from_behind(moving, "seq", -1)
        return (moving, summed + moving)

    return lax.fori_loop(
        0, lax.axis_size("seq") - 1, backward_relay_turn, (own_total, empty_state)
    )[1]


def per_device(queries, key_vectors, value_vectors, norm_gain, cotangent):
    tokens_here, features = queries.shape
    head_count = features // HD
    block_rows = min(512, tokens_here)
    block_count = tokens_here // block_rows
    block_shape = (block_count, block_rows, head_count, HD)
    query_blocks = queries.reshape(block_shape)
    key_blocks = key_vectors.reshape(block_shape)
    value_blocks = value_vectors.reshape(block_shape)
    positions = jnp.arange(block_rows)
    causal = positions[:, None] >= positions[None, :]
    local_kv = jnp.einsum(
        "nshd,nshe->nhde", key_blocks, value_blocks, preferred_element_type=jnp.float32
    )
    incoming = forward_prefix(jnp.sum(local_kv, axis=0))
    running = jnp.cumsum(local_kv, axis=0)
    prefix_state = incoming[None] + jnp.concatenate(
        [jnp.zeros_like(local_kv), running[:-1]], axis=0
    )
    prefix_low = prefix_state.astype(jnp.bfloat16)
    scores = jnp.einsum(
        "nthd,nshd->nhts", query_blocks, key_blocks, preferred_element_type=jnp.float32
    )
    block_weights = jnp.where(causal, scores, 0.0).astype(jnp.bfloat16)
    attended = jnp.einsum(
        "nthd,nhde->nthe", query_blocks, prefix_low, preferred_element_type=jnp.float32
    )
    attended = attended + jnp.einsum(
        "nhts,nshe->nthe", block_weights, value_blocks, preferred_element_type=jnp.float32
    )
    attended = attended.reshape(tokens_here, features)
    scaled_grad = cotangent.astype(jnp.float32) * norm_gain
    squares, inner = lax.psum(
        (jnp.sum(attended * attended, axis=1), jnp.sum(scaled_grad * attended, axis=1)), "head"
    )
    inverse_rms = lax.rsqrt(squares / FEAT + EPS)[:, None]
    inner = inner[:, None]
    layer_out = (attended * inverse_rms * norm_gain).astype(jnp.bfloat16)
    out_grad = (
        inverse_rms * (scaled_grad - attended * inner * inverse_rms * inverse_rms / FEAT)
    ).astype(jnp.bfloat16)
    grad_blocks = out_grad.reshape(block_shape)
    local_qg = jnp.einsum(
        "nthd,nthe->nhde", query_blocks, grad_blocks, preferred_element_type=jnp.float32
    )
    later_states = backward_suffix(jnp.sum(local_qg, axis=0))
    running_back = jnp.cumsum(local_qg[::-1], axis=0)[::-1]
    suffix_state = later_states[None] + jnp.concatenate(
        [running_back[1:], jnp.zeros_like(local_qg)], axis=0
    )
    suffix_low = suffix_state.astype(jnp.bfloat16)
    grad_scores = jnp.einsum(
        "nthe,nshe->nhts", grad_blocks, value_blocks, preferred_element_type=jnp.float32
    )
    grad_weights = jnp.where(causal, grad_scores, 0.0).astype(jnp.bfloat16)
    query_grad = jnp.einsum(
        "nthe,nhde->nthd", grad_blocks, prefix_low, preferred_element_type=jnp.float32
    )
    query_grad = query_grad + jnp.einsum(
        "nhts,nshd->nthd", grad_weights, key_blocks, preferred_element_type=jnp.float32
    )
    key_grad = jnp.einsum(
        "nshe,nhde->nshd", value_blocks, suffix_low, preferred_element_type=jnp.float32
    )
    key_grad = key_grad + jnp.einsum(
        "nhts,nthd->nshd", grad_weights, query_blocks, preferred_element_type=jnp.float32
    )
    value_grad = jnp.einsum(
        "nshd,nhde->nshe", key_blocks, suffix_low, preferred_element_type=jnp.float32
    )
    value_grad = value_grad + jnp.einsum(
        "nhts,nthe->nshe", block_weights, grad_blocks, preferred_element_type=jnp.float32
    )
    grad_query = query_grad.reshape(tokens_here, features).astype(jnp.bfloat16)
    grad_key = key_grad.reshape(tokens_here, features).astype(jnp.bfloat16)
    grad_value = value_grad.reshape(tokens_here, features).astype(jnp.bfloat16)
    return (layer_out, grad_query, grad_key, grad_value)


def solution(mesh):
    return jax.shard_map(
        per_device,
        mesh=mesh,
        in_specs=(
            P(("dp", "seq"), "head"),
            P(("dp", "seq"), "head"),
            P(("dp", "seq"), "head"),
            P("head"),
            P(("dp", "seq"), "head"),
        ),
        out_specs=(
            P(("dp", "seq"), "head"),
            P(("dp", "seq"), "head"),
            P(("dp", "seq"), "head"),
            P(("dp", "seq"), "head"),
        ),
        check_vma=False,
    )
```

profile of v0, /device:TPU:22, one launch (start us, length us, event | category | flops | bytes accessed | tf_op | source)
XLA Modules:
  0.0 538.4 jit_solution(9351575457497056380)
XLA Ops:
  7.6 242.4 %while.26 = (s32[]{:T(128)}, f32[4,128,128]{2,1,0:T(8,128)S(1)}, f32[4,128,128]{2,1,0:T(8,128)S(1)}, s32[]{:T(128)}, s32[]{:T(128)}) while((s32[]{:T(128)}, f32[4,128,128]{2,1,0:T(8,128)S(1)}, f32[4,128,128]{2,1,0:T(8,128)S(1)}, s32[]{:T(128)}, s32[]{:T(128)}) %tuple.47), condition=%wide.region_1.0_spmd.clone, body=%wide.region_0.0_spmd.clone.sunk | while | flops 131075 | bytes 2359407 | solution.py:27
  13.6 11.5 %collective-permute-done = f32[4,128,128]{2,1,0:T(8,128)S(1)} collective-permute-done((f32[4,128,128]{2,1,0:T(8,128)S(1)}, f32[4,128,128]{2,1,0:T(8,128)S(1)}, u32[]{:S(2)}, u32[]{:S(2)}) %collective-permute-start) | collective-permute-done | bytes 262176 | tf_op jit(solution)/shard_map/while/body/eval_jaxpr/ppermute | solution.py:16
  32.2 11.1 %collective-permute-done = f32[4,128,128]{2,1,0:T(8,128)S(1)} collective-permute-done((f32[4,128,128]{2,1,0:T(8,128)S(1)}, f32[4,128,128]{2,1,0:T(8,128)S(1)}, u32[]{:S(2)}, u32[]{:S(2)}) %collective-permute-start) | collective-permute-done | bytes 262176 | tf_op jit(solution)/shard_map/while/body/eval_jaxpr/ppermute | solution.py:16
  49.1 13.5 %collective-permute-done = f32[4,128,128]{2,1,0:T(8,128)S(1)} collective-permute-done((f32[4,128,128]{2,1,0:T(8,128)S(1)}, f32[4,128,128]{2,1,0:T(8,128)S(1)}, u32[]{:S(2)}, u32[]{:S(2)}) %collective-permute-start) | collective-permute-done | bytes 262176 | tf_op jit(solution)/shard_map/while/body/eval_jaxpr/ppermute | solution.py:16
  64.6 16.1 %collective-permute-done = f32[4,128,128]{2,1,0:T(8,128)S(1)} collective-permute-done((f32[4,128,128]{2,1,0:T(8,128)S(1)}, f32[4,128,128]{2,1,0:T(8,128)S(1)}, u32[]{:S(2)}, u32[]{:S(2)}) %collective-permute-start) | collective-permute-done | bytes 262176 | tf_op jit(solution)/shard_map/while/body/eval_jaxpr/ppermute | solution.py:16
  82.8 12.5 %collective-permute-done = f32[4,128,128]{2,1,0:T(8,128)S(1)} collective-permute-done((f32[4,128,128]{2,1,0:T(8,128)S(1)}, f32[4,128,128]{2,1,0:T(8,128)S(1)}, u32[]{:S(2)}, u32[]{:S(2)}) %collective-permute-start) | collective-permute-done | bytes 262176 | tf_op jit(solution)/shard_map/while/body/eval_jaxpr/ppermute | solution.py:16
  97.3 13.3 %collective-permute-done = f32[4,128,128]{2,1,0:T(8,128)S(1)} collective-permute-done((f32[4,128,128]{2,1,0:T(8,128)S(1)}, f32[4,128,128]{2,1,0:T(8,128)S(1)}, u32[]{:S(2)}, u32[]{:S(2)}) %collective-permute-start) | collective-permute-done | bytes 262176 | tf_op jit(solution)/shard_map/while/body/eval_jaxpr/ppermute | solution.py:16
  112.6 11.9 %collective-permute-done = f32[4,128,128]{2,1,0:T(8,128)S(1)} collective-permute-done((f32[4,128,128]{2,1,0:T(8,128)S(1)}, f32[4,128,128]{2,1,0:T(8,128)S(1)}, u32[]{:S(2)}, u32[]{:S(2)}) %collective-permute-start) | collective-permute-done | bytes 262176 | tf_op jit(solution)/shard_map/while/body/eval_jaxpr/ppermute | solution.py:16
  126.6 13.7 %collective-permute-done = f32[4,128,128]{2,1,0:T(8,128)S(1)} collective-permute-done((f32[4,128,128]{2,1,0:T(8,128)S(1)}, f32[4,128,128]{2,1,0:T(8,128)S(1)}, u32[]{:S(2)}, u32[]{:S(2)}) %collective-permute-start) | collective-permute-done | bytes 262176 | tf_op jit(solution)/shard_map/while/body/eval_jaxpr/ppermute | solution.py:16
  142.3 11.7 %collective-permute-done = f32[4,128,128]{2,1,0:T(8,128)S(1)} collective-permute-done((f32[4,128,128]{2,1,0:T(8,128)S(1)}, f32[4,128,128]{2,1,0:T(8,128)S(1)}, u32[]{:S(2)}, u32[]{:S(2)}) %collective-permute-start) | collective-permute-done | bytes 262176 | tf_op jit(solution)/shard_map/while/body/eval_jaxpr/ppermute | solution.py:16
  178.9 14.6 %collective-permute-done = f32[4,128,128]{2,1,0:T(8,128)S(1)} collective-permute-done((f32[4,128,128]{2,1,0:T(8,128)S(1)}, f32[4,128,128]{2,1,0:T(8,128)S(1)}, u32[]{:S(2)}, u32[]{:S(2)}) %collective-permute-start) | collective-permute-done | bytes 262176 | tf_op jit(solution)/shard_map/while/body/eval_jaxpr/ppermute | solution.py:16
  195.6 19.8 %collective-permute-done = f32[4,128,128]{2,1,0:T(8,128)S(1)} collective-permute-done((f32[4,128,128]{2,1,0:T(8,128)S(1)}, f32[4,128,128]{2,1,0:T(8,128)S(1)}, u32[]{:S(2)}, u32[]{:S(2)}) %collective-permute-start) | collective-permute-done | bytes 262176 | tf_op jit(solution)/shard_map/while/body/eval_jaxpr/ppermute | solution.py:16
  217.4 15.2 %collective-permute-done = f32[4,128,128]{2,1,0:T(8,128)S(1)} collective-permute-done((f32[4,128,128]{2,1,0:T(8,128)S(1)}, f32[4,128,128]{2,1,0:T(8,128)S(1)}, u32[]{:S(2)}, u32[]{:S(2)}) %collective-permute-start) | collective-permute-done | bytes 262176 | tf_op jit(solution)/shard_map/while/body/eval_jaxpr/ppermute | solution.py:16
  234.6 15.2 %collective-permute-done = f32[4,128,128]{2,1,0:T(8,128)S(1)} collective-permute-done((f32[4,128,128]{2,1,0:T(8,128)S(1)}, f32[4,128,128]{2,1,0:T(8,128)S(1)}, u32[]{:S(2)}, u32[]{:S(2)}) %collective-permute-start) | collective-permute-done | bytes 262176 | tf_op jit(solution)/shard_map/while/body/eval_jaxpr/ppermute | solution.py:16
  252.0 21.1 %all-reduce = (f32[512]{0:T(512)S(1)}, f32[512]{0:T(512)S(1)}) all-reduce(f32[512]{0:T(512)S(1)} %get-tuple-element.87, f32[512]{0:T(512)S(1)} %multiply_reduce_fusion), channel_id=1, replica_groups=mesh['seq'=16,'head'=8,'dp'=4] {'head'}, use_global_device_ids=true, to_apply=%region_3.0 | all-reduce | flops 1024 | bytes 8192 | tf_op jit(solution)/shard_map/psum | solution.py:77
  278.3 249.9 %while.27 = (s32[]{:T(128)}, f32[4,128,128]{2,1,0:T(8,128)S(1)}, f32[4,128,128]{2,1,0:T(8,128)S(1)}, s32[]{:T(128)}, s32[]{:T(128)}) while((s32[]{:T(128)}, f32[4,128,128]{2,1,0:T(8,128)S(1)}, f32[4,128,128]{2,1,0:T(8,128)S(1)}, s32[]{:T(128)}, s32[]{:T(128)}) %tuple.50), condition=%wide.region_7.8_spmd.clone, body=%wide.region_6.7_spmd.clone.sunk | while | flops 131075 | bytes 2359407 | solution.py:40
  280.4 10.7 %collective-permute-done.1 = f32[4,128,128]{2,1,0:T(8,128)S(1)} collective-permute-done((f32[4,128,128]{2,1,0:T(8,128)S(1)}, f32[4,128,128]{2,1,0:T(8,128)S(1)}, u32[]{:S(2)}, u32[]{:S(2)}) %collective-permute-start.1) | collective-permute-done | bytes 262176 | tf_op jit(solution)/shard_map/while/body/eval_jaxpr/ppermute | solution.py:16
  316.7 11.6 %collective-permute-done.1 = f32[4,128,128]{2,1,0:T(8,128)S(1)} collective-permute-done((f32[4,128,128]{2,1,0:T(8,128)S(1)}, f32[4,128,128]{2,1,0:T(8,128)S(1)}, u32[]{:S(2)}, u32[]{:S(2)}) %collective-permute-start.1) | collective-permute-done | bytes 262176 | tf_op jit(solution)/shard_map/while/body/eval_jaxpr/ppermute | solution.py:16
  345.0 11.1 %collective-permute-start.1 = (f32[4,128,128]{2,1,0:T(8,128)S(1)}, f32[4,128,128]{2,1,0:T(8,128)S(1)}, u32[]{:S(2)}, u32[]{:S(2)}) collective-permute-start(f32[4,128,128]{2,1,0:T(8,128)S(1)} %get-tuple-element.148), channel_id=1, source_target_pairs={{32,0},{64,32},{96,64},{128,96},{160,128},{192,160},{224,192},{256... | collective-permute-start | bytes 786440 | tf_op jit(solution)/shard_map/while/body/eval_jaxpr/ppermute | solution.py:16
  356.0 10.5 %collective-permute-done.1 = f32[4,128,128]{2,1,0:T(8,128)S(1)} collective-permute-done((f32[4,128,128]{2,1,0:T(8,128)S(1)}, f32[4,128,128]{2,1,0:T(8,128)S(1)}, u32[]{:S(2)}, u32[]{:S(2)}) %collective-permute-start.1) | collective-permute-done | bytes 262176 | tf_op jit(solution)/shard_map/while/body/eval_jaxpr/ppermute | solution.py:16
  390.8 10.1 %collective-permute-done.1 = f32[4,128,128]{2,1,0:T(8,128)S(1)} collective-permute-done((f32[4,128,128]{2,1,0:T(8,128)S(1)}, f32[4,128,128]{2,1,0:T(8,128)S(1)}, u32[]{:S(2)}, u32[]{:S(2)}) %collective-permute-start.1) | collective-permute-done | bytes 262176 | tf_op jit(solution)/shard_map/while/body/eval_jaxpr/ppermute | solution.py:16
  408.5 9.8 %collective-permute-done.1 = f32[4,128,128]{2,1,0:T(8,128)S(1)} collective-permute-done((f32[4,128,128]{2,1,0:T(8,128)S(1)}, f32[4,128,128]{2,1,0:T(8,128)S(1)}, u32[]{:S(2)}, u32[]{:S(2)}) %collective-permute-start.1) | collective-permute-done | bytes 262176 | tf_op jit(solution)/shard_map/while/body/eval_jaxpr/ppermute | solution.py:16
  458.4 12.1 %collective-permute-done.1 = f32[4,128,128]{2,1,0:T(8,128)S(1)} collective-permute-done((f32[4,128,128]{2,1,0:T(8,128)S(1)}, f32[4,128,128]{2,1,0:T(8,128)S(1)}, u32[]{:S(2)}, u32[]{:S(2)}) %collective-permute-start.1) | collective-permute-done | bytes 262176 | tf_op jit(solution)/shard_map/while/body/eval_jaxpr/ppermute | solution.py:16
  478.0 11.2 %collective-permute-done.1 = f32[4,128,128]{2,1,0:T(8,128)S(1)} collective-permute-done((f32[4,128,128]{2,1,0:T(8,128)S(1)}, f32[4,128,128]{2,1,0:T(8,128)S(1)}, u32[]{:S(2)}, u32[]{:S(2)}) %collective-permute-start.1) | collective-permute-done | bytes 262176 | tf_op jit(solution)/shard_map/while/body/eval_jaxpr/ppermute | solution.py:16
  (149 shorter events, 248.2 us)
Async XLA Ops:
  7.6 17.6 %collective-permute-start = (f32[4,128,128]{2,1,0:T(8,128)S(1)}, f32[4,128,128]{2,1,0:T(8,128)S(1)}, u32[]{:S(2)}, u32[]{:S(2)}) collective-permute-start(f32[4,128,128]{2,1,0:T(8,128)S(1)} %get-tuple-element.133), channel_id=1, source_target_pairs={{0,32},{32,64},{64,96},{96,128},{128,160},{160,192},{192,224},{224... | collective-permute-start | bytes 786440 | tf_op jit(solution)/shard_map/while/body/eval_jaxpr/ppermute | solution.py:16
  25.3 18.0 %collective-permute-start = (f32[4,128,128]{2,1,0:T(8,128)S(1)}, f32[4,128,128]{2,1,0:T(8,128)S(1)}, u32[]{:S(2)}, u32[]{:S(2)}) collective-permute-start(f32[4,128,128]{2,1,0:T(8,128)S(1)} %get-tuple-element.133), channel_id=1, source_target_pairs={{0,32},{32,64},{64,96},{96,128},{128,160},{160,192},{192,224},{224... | collective-permute-start | bytes 786440 | tf_op jit(solution)/shard_map/while/body/eval_jaxpr/ppermute | solution.py:16
  43.4 19.2 %collective-permute-start = (f32[4,128,128]{2,1,0:T(8,128)S(1)}, f32[4,128,128]{2,1,0:T(8,128)S(1)}, u32[]{:S(2)}, u32[]{:S(2)}) collective-permute-start(f32[4,128,128]{2,1,0:T(8,128)S(1)} %get-tuple-element.133), channel_id=1, source_target_pairs={{0,32},{32,64},{64,96},{96,128},{128,160},{160,192},{192,224},{224... | collective-permute-start | bytes 786440 | tf_op jit(solution)/shard_map/while/body/eval_jaxpr/ppermute | solution.py:16
  62.7 18.0 %collective-permute-start = (f32[4,128,128]{2,1,0:T(8,128)S(1)}, f32[4,128,128]{2,1,0:T(8,128)S(1)}, u32[]{:S(2)}, u32[]{:S(2)}) collective-permute-start(f32[4,128,128]{2,1,0:T(8,128)S(1)} %get-tuple-element.133), channel_id=1, source_target_pairs={{0,32},{32,64},{64,96},{96,128},{128,160},{160,192},{192,224},{224... | collective-permute-start | bytes 786440 | tf_op jit(solution)/shard_map/while/body/eval_jaxpr/ppermute | solution.py:16
  80.8 14.4 %collective-permute-start = (f32[4,128,128]{2,1,0:T(8,128)S(1)}, f32[4,128,128]{2,1,0:T(8,128)S(1)}, u32[]{:S(2)}, u32[]{:S(2)}) collective-permute-start(f32[4,128,128]{2,1,0:T(8,128)S(1)} %get-tuple-element.133), channel_id=1, source_target_pairs={{0,32},{32,64},{64,96},{96,128},{128,160},{160,192},{192,224},{224... | collective-permute-start | bytes 786440 | tf_op jit(solution)/shard_map/while/body/eval_jaxpr/ppermute | solution.py:16
  95.4 15.2 %collective-permute-start = (f32[4,128,128]{2,1,0:T(8,128)S(1)}, f32[4,128,128]{2,1,0:T(8,128)S(1)}, u32[]{:S(2)}, u32[]{:S(2)}) collective-permute-start(f32[4,128,128]{2,1,0:T(8,128)S(1)} %get-tuple-element.133), channel_id=1, source_target_pairs={{0,32},{32,64},{64,96},{96,128},{128,160},{160,192},{192,224},{224... | collective-permute-start | bytes 786440 | tf_op jit(solution)/shard_map/while/body/eval_jaxpr/ppermute | solution.py:16
  110.7 13.8 %collective-permute-start = (f32[4,128,128]{2,1,0:T(8,128)S(1)}, f32[4,128,128]{2,1,0:T(8,128)S(1)}, u32[]{:S(2)}, u32[]{:S(2)}) collective-permute-start(f32[4,128,128]{2,1,0:T(8,128)S(1)} %get-tuple-element.133), channel_id=1, source_target_pairs={{0,32},{32,64},{64,96},{96,128},{128,160},{160,192},{192,224},{224... | collective-permute-start | bytes 786440 | tf_op jit(solution)/shard_map/while/body/eval_jaxpr/ppermute | solution.py:16
  124.6 15.6 %collective-permute-start = (f32[4,128,128]{2,1,0:T(8,128)S(1)}, f32[4,128,128]{2,1,0:T(8,128)S(1)}, u32[]{:S(2)}, u32[]{:S(2)}) collective-permute-start(f32[4,128,128]{2,1,0:T(8,128)S(1)} %get-tuple-element.133), channel_id=1, source_target_pairs={{0,32},{32,64},{64,96},{96,128},{128,160},{160,192},{192,224},{224... | collective-permute-start | bytes 786440 | tf_op jit(solution)/shard_map/while/body/eval_jaxpr/ppermute | solution.py:16
  177.0 16.6 %collective-permute-start = (f32[4,128,128]{2,1,0:T(8,128)S(1)}, f32[4,128,128]{2,1,0:T(8,128)S(1)}, u32[]{:S(2)}, u32[]{:S(2)}) collective-permute-start(f32[4,128,128]{2,1,0:T(8,128)S(1)} %get-tuple-element.133), channel_id=1, source_target_pairs={{0,32},{32,64},{64,96},{96,128},{128,160},{160,192},{192,224},{224... | collective-permute-start | bytes 786440 | tf_op jit(solution)/shard_map/while/body/eval_jaxpr/ppermute | solution.py:16
  193.7 21.7 %collective-permute-start = (f32[4,128,128]{2,1,0:T(8,128)S(1)}, f32[4,128,128]{2,1,0:T(8,128)S(1)}, u32[]{:S(2)}, u32[]{:S(2)}) collective-permute-start(f32[4,128,128]{2,1,0:T(8,128)S(1)} %get-tuple-element.133), channel_id=1, source_target_pairs={{0,32},{32,64},{64,96},{96,128},{128,160},{160,192},{192,224},{224... | collective-permute-start | bytes 786440 | tf_op jit(solution)/shard_map/while/body/eval_jaxpr/ppermute | solution.py:16
  215.5 17.1 %collective-permute-start = (f32[4,128,128]{2,1,0:T(8,128)S(1)}, f32[4,128,128]{2,1,0:T(8,128)S(1)}, u32[]{:S(2)}, u32[]{:S(2)}) collective-permute-start(f32[4,128,128]{2,1,0:T(8,128)S(1)} %get-tuple-element.133), channel_id=1, source_target_pairs={{0,32},{32,64},{64,96},{96,128},{128,160},{160,192},{192,224},{224... | collective-permute-start | bytes 786440 | tf_op jit(solution)/shard_map/while/body/eval_jaxpr/ppermute | solution.py:16
  232.7 17.2 %collective-permute-start = (f32[4,128,128]{2,1,0:T(8,128)S(1)}, f32[4,128,128]{2,1,0:T(8,128)S(1)}, u32[]{:S(2)}, u32[]{:S(2)}) collective-permute-start(f32[4,128,128]{2,1,0:T(8,128)S(1)} %get-tuple-element.133), channel_id=1, source_target_pairs={{0,32},{32,64},{64,96},{96,128},{128,160},{160,192},{192,224},{224... | collective-permute-start | bytes 786440 | tf_op jit(solution)/shard_map/while/body/eval_jaxpr/ppermute | solution.py:16
  291.2 16.7 %collective-permute-start.1 = (f32[4,128,128]{2,1,0:T(8,128)S(1)}, f32[4,128,128]{2,1,0:T(8,128)S(1)}, u32[]{:S(2)}, u32[]{:S(2)}) collective-permute-start(f32[4,128,128]{2,1,0:T(8,128)S(1)} %get-tuple-element.148), channel_id=1, source_target_pairs={{32,0},{64,32},{96,64},{128,96},{160,128},{192,160},{224,192},{256... | collective-permute-start | bytes 786440 | tf_op jit(solution)/shard_map/while/body/eval_jaxpr/ppermute | solution.py:16
  308.1 20.2 %collective-permute-start.1 = (f32[4,128,128]{2,1,0:T(8,128)S(1)}, f32[4,128,128]{2,1,0:T(8,128)S(1)}, u32[]{:S(2)}, u32[]{:S(2)}) collective-permute-start(f32[4,128,128]{2,1,0:T(8,128)S(1)} %get-tuple-element.148), channel_id=1, source_target_pairs={{32,0},{64,32},{96,64},{128,96},{160,128},{192,160},{224,192},{256... | collective-permute-start | bytes 786440 | tf_op jit(solution)/shard_map/while/body/eval_jaxpr/ppermute | solution.py:16
  328.4 16.5 %collective-permute-start.1 = (f32[4,128,128]{2,1,0:T(8,128)S(1)}, f32[4,128,128]{2,1,0:T(8,128)S(1)}, u32[]{:S(2)}, u32[]{:S(2)}) collective-permute-start(f32[4,128,128]{2,1,0:T(8,128)S(1)} %get-tuple-element.148), channel_id=1, source_target_pairs={{32,0},{64,32},{96,64},{128,96},{160,128},{192,160},{224,192},{256... | collective-permute-start | bytes 786440 | tf_op jit(solution)/shard_map/while/body/eval_jaxpr/ppermute | solution.py:16
  345.0 21.6 %collective-permute-start.1 = (f32[4,128,128]{2,1,0:T(8,128)S(1)}, f32[4,128,128]{2,1,0:T(8,128)S(1)}, u32[]{:S(2)}, u32[]{:S(2)}) collective-permute-start(f32[4,128,128]{2,1,0:T(8,128)S(1)} %get-tuple-element.148), channel_id=1, source_target_pairs={{32,0},{64,32},{96,64},{128,96},{160,128},{192,160},{224,192},{256... | collective-permute-start | bytes 786440 | tf_op jit(solution)/shard_map/while/body/eval_jaxpr/ppermute | solution.py:16
  366.7 16.6 %collective-permute-start.1 = (f32[4,128,128]{2,1,0:T(8,128)S(1)}, f32[4,128,128]{2,1,0:T(8,128)S(1)}, u32[]{:S(2)}, u32[]{:S(2)}) collective-permute-start(f32[4,128,128]{2,1,0:T(8,128)S(1)} %get-tuple-element.148), channel_id=1, source_target_pairs={{32,0},{64,32},{96,64},{128,96},{160,128},{192,160},{224,192},{256... | collective-permute-start | bytes 786440 | tf_op jit(solution)/shard_map/while/body/eval_jaxpr/ppermute | solution.py:16
  383.4 17.5 %collective-permute-start.1 = (f32[4,128,128]{2,1,0:T(8,128)S(1)}, f32[4,128,128]{2,1,0:T(8,128)S(1)}, u32[]{:S(2)}, u32[]{:S(2)}) collective-permute-start(f32[4,128,128]{2,1,0:T(8,128)S(1)} %get-tuple-element.148), channel_id=1, source_target_pairs={{32,0},{64,32},{96,64},{128,96},{160,128},{192,160},{224,192},{256... | collective-permute-start | bytes 786440 | tf_op jit(solution)/shard_map/while/body/eval_jaxpr/ppermute | solution.py:16
  401.0 17.3 %collective-permute-start.1 = (f32[4,128,128]{2,1,0:T(8,128)S(1)}, f32[4,128,128]{2,1,0:T(8,128)S(1)}, u32[]{:S(2)}, u32[]{:S(2)}) collective-permute-start(f32[4,128,128]{2,1,0:T(8,128)S(1)} %get-tuple-element.148), channel_id=1, source_target_pairs={{32,0},{64,32},{96,64},{128,96},{160,128},{192,160},{224,192},{256... | collective-permute-start | bytes 786440 | tf_op jit(solution)/shard_map/while/body/eval_jaxpr/ppermute | solution.py:16
  418.4 16.7 %collective-permute-start.1 = (f32[4,128,128]{2,1,0:T(8,128)S(1)}, f32[4,128,128]{2,1,0:T(8,128)S(1)}, u32[]{:S(2)}, u32[]{:S(2)}) collective-permute-start(f32[4,128,128]{2,1,0:T(8,128)S(1)} %get-tuple-element.148), channel_id=1, source_target_pairs={{32,0},{64,32},{96,64},{128,96},{160,128},{192,160},{224,192},{256... | collective-permute-start | bytes 786440 | tf_op jit(solution)/shard_map/while/body/eval_jaxpr/ppermute | solution.py:16
  435.1 17.0 %collective-permute-start.1 = (f32[4,128,128]{2,1,0:T(8,128)S(1)}, f32[4,128,128]{2,1,0:T(8,128)S(1)}, u32[]{:S(2)}, u32[]{:S(2)}) collective-permute-start(f32[4,128,128]{2,1,0:T(8,128)S(1)} %get-tuple-element.148), channel_id=1, source_target_pairs={{32,0},{64,32},{96,64},{128,96},{160,128},{192,160},{224,192},{256... | collective-permute-start | bytes 786440 | tf_op jit(solution)/shard_map/while/body/eval_jaxpr/ppermute | solution.py:16
  452.3 18.1 %collective-permute-start.1 = (f32[4,128,128]{2,1,0:T(8,128)S(1)}, f32[4,128,128]{2,1,0:T(8,128)S(1)}, u32[]{:S(2)}, u32[]{:S(2)}) collective-permute-start(f32[4,128,128]{2,1,0:T(8,128)S(1)} %get-tuple-element.148), channel_id=1, source_target_pairs={{32,0},{64,32},{96,64},{128,96},{160,128},{192,160},{224,192},{256... | collective-permute-start | bytes 786440 | tf_op jit(solution)/shard_map/while/body/eval_jaxpr/ppermute | solution.py:16
  470.6 18.6 %collective-permute-start.1 = (f32[4,128,128]{2,1,0:T(8,128)S(1)}, f32[4,128,128]{2,1,0:T(8,128)S(1)}, u32[]{:S(2)}, u32[]{:S(2)}) collective-permute-start(f32[4,128,128]{2,1,0:T(8,128)S(1)} %get-tuple-element.148), channel_id=1, source_target_pairs={{32,0},{64,32},{96,64},{128,96},{160,128},{192,160},{224,192},{256... | collective-permute-start | bytes 786440 | tf_op jit(solution)/shard_map/while/body/eval_jaxpr/ppermute | solution.py:16
  489.3 14.4 %collective-permute-start.1 = (f32[4,128,128]{2,1,0:T(8,128)S(1)}, f32[4,128,128]{2,1,0:T(8,128)S(1)}, u32[]{:S(2)}, u32[]{:S(2)}) collective-permute-start(f32[4,128,128]{2,1,0:T(8,128)S(1)} %get-tuple-element.148), channel_id=1, source_target_pairs={{32,0},{64,32},{96,64},{128,96},{160,128},{192,160},{224,192},{256... | collective-permute-start | bytes 786440 | tf_op jit(solution)/shard_map/while/body/eval_jaxpr/ppermute | solution.py:16
  (18 other events, 619.9 us)
where the time goes:
time: 540 us; the launch traced here: 538 us
  waiting for transfers between devices  337 us (62%)
  starting transfers between devices  151 us (28%)
  blocking collectives  21.1 us (4%)
  matrix products  12 us (2%)
  local copies, waits for them, and re-layouts  8.87 us (2%)
  other arithmetic  5.93 us (1%)
    ppermute x30, waiting for transfers between devices, from_behind(): return lax.ppermute(block, axis, route)  337 us
    ppermute x30, starting transfers between devices, from_behind(): return lax.ppermute(block, axis, route)  151 us
    psum x1, blocking collectives, per_device(): lax.psum((jnp.sum(attended * attended, axis=1), jnp.sum(scaled_grad * att...  21.1 us
  transfers between devices with their start and end apart: 30, of which 30 were waited for; matrix products, arithmetic and copies ran while one was open for 0% of the time, Pallas kernels for 0%

commit v1 on v0

v1 whole, which is shorter than its diff:
```python
import jax
import jax.numpy as jnp
from jax import lax
from jax.experimental import pallas as pl
from jax.experimental.pallas import tpu as pltpu
from jax.sharding import PartitionSpec as P

HD = 128
FEAT = 4096
EPS = 1e-06
F32 = jnp.float32
BF16 = jnp.bfloat16
VMEM_LIMIT = 24 * 1024 * 1024


def dot(a, b, contract):
    return lax.dot_general(a, b, ((contract[0], contract[1]), ((), ())), preferred_element_type=F32)


def nn(a, b):
    return dot(a, b, ((1,), (0,)))


def nt(a, b):
    return dot(a, b, ((1,), (1,)))


def tn(a, b):
    return dot(a, b, ((0,), (0,)))


def head_columns(h):
    return slice(h * HD, (h + 1) * HD)


def call(kernel, out_shape, flops, bytes_accessed, *operands):
    return pl.pallas_call(
        kernel,
        out_shape=out_shape,
        compiler_params=pltpu.CompilerParams(vmem_limit_bytes=VMEM_LIMIT),
        cost_estimate=pl.CostEstimate(
            flops=flops, bytes_accessed=bytes_accessed, transcendentals=0
        ),
    )(*operands)


def shape_of(shape, dtype=F32):
    return jax.ShapeDtypeStruct(shape, dtype)


def state_of_heads(ref, heads):
    return ref[...].reshape(heads, HD, HD)


def outer_kernel(heads, a_ref, b_ref, state_ref):
    per_head = state_ref.shape[0] // heads
    rows = state_ref.shape[1]
    for h in range(heads):
        cols = head_columns(h)
        state = tn(a_ref[:, cols], b_ref[:, cols])
        state_ref[h * per_head : (h + 1) * per_head] = state.reshape(per_head, rows, HD)


def prefix_kernel(part_ref, out_ref):
    n = part_ref.shape[0]
    total = jnp.zeros(part_ref.shape[1:], F32)
    for m in range(n):
        out_ref[m] = total
        if m < n - 1:
            total = total + part_ref[m]


def suffix_kernel(part_ref, out_ref):
    n = part_ref.shape[0]
    total = jnp.zeros(part_ref.shape[1:], F32)
    for m in reversed(range(n)):
        out_ref[m] = total
        if m > 0:
            total = total + part_ref[m]


def masked(block):
    t = lax.broadcasted_iota(jnp.int32, block.shape, 0)
    s = lax.broadcasted_iota(jnp.int32, block.shape, 1)
    return jnp.where(t >= s, block, 0.0).astype(BF16)


def local_kernel(heads, q_ref, k_ref, v_ref, w_ref, l_ref):
    for h in range(heads):
        cols = head_columns(h)
        weights = masked(nt(q_ref[:, cols], k_ref[:, cols]))
        w_ref[h] = weights
        l_ref[:, cols] = nn(weights, v_ref[:, cols])


def attend_kernel(heads, q_ref, p_ref, l_ref, c_ref, g_ref, a_ref, sums_ref):
    state = state_of_heads(p_ref, heads).astype(BF16)
    squares = jnp.zeros((q_ref.shape[0], HD), F32)
    inner = jnp.zeros((q_ref.shape[0], HD), F32)
    for h in range(heads):
        cols = head_columns(h)
        attended = nn(q_ref[:, cols], state[h]) + l_ref[:, cols]
        a_ref[:, cols] = attended
        scaled = c_ref[:, cols].astype(F32) * g_ref[:, cols]
        squares = squares + attended * attended
        inner = inner + scaled * attended
    squares = jnp.sum(squares.T, axis=0, keepdims=True)
    inner = jnp.sum(inner.T, axis=0, keepdims=True)
    both = jnp.concatenate([squares, inner], axis=0)
    for i in range(sums_ref.shape[0]):
        sums_ref[i] = both


def norm_kernel(heads, s_ref, a_ref, c_ref, g_ref, q_ref, o_ref, d_ref, state_ref):
    sums = s_ref[0]
    for i in range(1, s_ref.shape[0]):
        sums = sums + s_ref[i]
    inverse = lax.rsqrt(sums[0:1] / FEAT + EPS)
    slope = sums[1:2] * inverse * inverse / FEAT
    rows = jnp.concatenate(
        [jnp.broadcast_to(inverse, (64, inverse.shape[1])), jnp.broadcast_to(slope, (64, slope.shape[1]))],
        axis=0,
    ).T
    inverse = rows[:, 0:1]
    slope = rows[:, 64:65]
    per_head = state_ref.shape[0] // heads
    for h in range(heads):
        cols = head_columns(h)
        attended = a_ref[:, cols]
        gain = g_ref[:, cols]
        scaled = c_ref[:, cols].astype(F32) * gain
        grad = (inverse * (scaled - attended * slope)).astype(BF16)
        d_ref[:, cols] = grad
        o_ref[:, cols] = (attended * inverse * gain).astype(BF16)
        state = tn(q_ref[:, cols], grad)
        state_ref[h * per_head : (h + 1) * per_head] = state.reshape(
            per_head, state_ref.shape[1], HD
        )


def grad_kernel(heads, d_ref, q_ref, k_ref, v_ref, w_ref, p_ref, gq_ref, gk_ref, gv_ref):
    state = state_of_heads(p_ref, heads).astype(BF16)
    for h in range(heads):
        cols = head_columns(h)
        grad = d_ref[:, cols]
        weights = masked(nt(grad, v_ref[:, cols]))
        gq_ref[:, cols] = (nt(grad, state[h]) + nn(weights, k_ref[:, cols])).astype(BF16)
        gk_ref[:, cols] = tn(weights, q_ref[:, cols])
        gv_ref[:, cols] = tn(w_ref[h], grad)


def final_kernel(heads, s_ref, k_ref, v_ref, gk_ref, gv_ref, key_ref, value_ref):
    state = state_of_heads(s_ref, heads).astype(BF16)
    for h in range(heads):
        cols = head_columns(h)
        key_ref[:, cols] = (nt(v_ref[:, cols], state[h]) + gk_ref[:, cols]).astype(BF16)
        value_ref[:, cols] = (nn(k_ref[:, cols], state[h]) + gv_ref[:, cols]).astype(BF16)


def exchange(parts, axis):
    return lax.all_to_all(parts, axis, 0, 0, tiled=True)


def per_device(queries, key_vectors, value_vectors, norm_gain, cotangent):
    tokens, features = queries.shape
    heads = features // HD
    seq = lax.axis_size("seq")
    head_devices = lax.axis_size("head")
    state_shape = (seq, heads * HD // seq, HD)
    wide = (tokens, features)
    gain = norm_gain.reshape(1, features)

    def bind(kernel):
        return lambda *refs: kernel(heads, *refs)

    product = 2 * tokens * features * HD
    square = 2 * tokens * tokens * features
    size = tokens * features

    with jax.named_scope("key_value_state"):
        local_kv = call(
            bind(outer_kernel), shape_of(state_shape), product, 5 * size, key_vectors, value_vectors
        )
    with jax.named_scope("prefix"):
        pieces = exchange(local_kv, "seq")
        sums = call(prefix_kernel, shape_of(state_shape), 0, size, pieces)
        prefix = exchange(sums, "seq")
    with jax.named_scope("inside_block"):
        weights, local = call(
            bind(local_kernel),
            (shape_of((heads, tokens, tokens), BF16), shape_of(wide)),
            2 * square,
            10 * size,
            queries,
            key_vectors,
            value_vectors,
        )
    with jax.named_scope("attended"):
        attended, sums = call(
            bind(attend_kernel),
            (shape_of(wide), shape_of((head_devices, 2, tokens))),
            product,
            12 * size,
            queries,
            prefix,
            local,
            cotangent,
            gain,
        )
        sums = exchange(sums, "head")
    with jax.named_scope("norm"):
        layer_out, out_grad, local_qg = call(
            bind(norm_kernel),
            (shape_of(wide, BF16), shape_of(wide, BF16), shape_of(state_shape)),
            product,
            12 * size,
            sums,
            attended,
            cotangent,
            gain,
            queries,
        )
    with jax.named_scope("suffix"):
        pieces = exchange(local_qg, "seq")
        sums = call(suffix_kernel, shape_of(state_shape), 0, size, pieces)
        suffix = exchange(sums, "seq")
    with jax.named_scope("grad_parts"):
        grad_query, key_part, value_part = call(
            bind(grad_kernel),
            (shape_of(wide, BF16), shape_of(wide), shape_of(wide)),
            4 * square,
            20 * size,
            out_grad,
            queries,
            key_vectors,
            value_vectors,
            weights,
            prefix,
        )
    with jax.named_scope("grads"):
        grad_key, grad_value = call(
            bind(final_kernel),
            (shape_of(wide, BF16), shape_of(wide, BF16)),
            2 * product,
            16 * size,
            suffix,
            key_vectors,
            value_vectors,
            key_part,
            value_part,
        )
    return (layer_out, grad_query, grad_key, grad_value)


def solution(mesh):
    split = P(("dp", "seq"), "head")
    return jax.shard_map(
        per_device,
        mesh=mesh,
        in_specs=(split, split, split, P("head"), split),
        out_specs=(split, split, split, split),
        check_vma=False,
    )
```

time: 540 us -> 97.1 us (0.18)
  the two profiles are of different devices: /device:TPU:22 before, /device:TPU:8 now
where the time goes in v1:
time: 97.1 us; the launch traced here: 96.5 us
  blocking collectives  55.3 us (57%)
  waiting for transfers between devices  14.9 us (15%)
  Pallas kernels  9.34 us (10%)
  local copies, waits for them, and re-layouts  9.12 us (9%)
  starting transfers between devices  7.07 us (7%)
    all_to_all x3, blocking collectives, exchange(): return lax.all_to_all(parts, axis, 0, 0, tiled=True)  55.3 us
    all_to_all x2, waiting for transfers between devices, exchange(): return lax.all_to_all(parts, axis, 0, 0, tiled=True)  14.9 us
    pallas_call x8, Pallas kernels, call(): pl.pallas_call(kernel, out_shape=out_shape, compiler_params=pltpu.Compile...  9.34 us
    unnamed x26, local copies, waits for them, and re-layouts  9.12 us
    all_to_all x2, starting transfers between devices, exchange(): return lax.all_to_all(parts, axis, 0, 0, tiled=True)  7.07 us
  transfers between devices with their start and end apart: 2, of which 2 were waited for; matrix products, arithmetic and copies ran while one was open for 0% of the time, Pallas kernels for 5%

profile of v1, /device:TPU:8, one launch (start us, length us, event | category | flops | bytes accessed | tf_op | source)
XLA Modules:
  0.0 96.5 jit_solution(1234990823385252449)
XLA Ops:
  0.7 1.1 %copy-done.1 = bf16[512,512]{1,0:T(8,128)(2,1)S(1)} copy-done((bf16[512,512]{1,0:T(8,128)(2,1)S(1)}, bf16[512,512]{1,0:T(8,128)(2,1)}, u32[]{:S(2)}) %copy-start.1) | copy-done | bytes 524312
  1.7 1.0 %copy-done.3 = bf16[512,512]{1,0:T(8,128)(2,1)S(1)} copy-done((bf16[512,512]{1,0:T(8,128)(2,1)S(1)}, bf16[512,512]{1,0:T(8,128)(2,1)}, u32[]{:S(2)}) %copy-start.3) | copy-done | bytes 524312
  2.8 0.3 key_value_state.1
  3.1 0.0 copy-start.7
  3.2 26.2 %all_to_all.25.part_ref = f32[16,32,128]{2,1,0:T(8,128)S(1)} all-to-all(f32[16,32,128]{2,1,0:T(8,128)S(1)} %key_value_state.1), channel_id=1, replica_groups=mesh['seq'=16,'head'=8,'dp'=4] {'seq'}, dimensions={0} | all-to-all | bytes 524288 | tf_op jit(solution)/shard_map/prefix/all_to_all | solution.py:161
  29.4 0.7 prefix.1
  30.1 3.5 %all-to-all-start.1 = ((f32[16,32,128]{2,1,0:T(8,128)}), f32[16,32,128]{2,1,0:T(8,128)S(1)}, u32[]{:S(2)}, u32[]{:S(2)}) async-start(f32[16,32,128]{2,1,0:T(8,128)} %prefix.1), calls=%async_computation.1 | async-start | bytes 524288 | tf_op jit(solution)/shard_map/prefix/all_to_all | solution.py:161
  33.7 1.3 %inside_block.1 = (bf16[4,512,512]{2,1,0:T(8,128)(2,1)S(1)}, f32[512,512]{1,0:T(8,128)S(1)}) custom-call(bf16[512,512]{1,0:T(8,128)(2,1)S(1)} %copy-done, bf16[512,512]{1,0:T(8,128)(2,1)S(1)} %copy-done.2, bf16[512,512]{1,0:T(8,128)(2,1)S(1)} %copy-done.4), custom_call_target="tpu_custom_call" | custom-call | flops 536870912 | bytes 2621440 | tf_op jit(solution)/shard_map/inside_block/pallas_call | solution.py:37
  35.0 1.3 %copy-done.5 = bf16[4,512,512]{2,1,0:T(8,128)(2,1)} copy-done((bf16[4,512,512]{2,1,0:T(8,128)(2,1)}, bf16[4,512,512]{2,1,0:T(8,128)(2,1)S(1)}, u32[]{:S(2)}) %copy-start.5) | copy-done | bytes 2097176
  36.4 9.3 %all-to-all-done.1.refs_1_.refs_5_ = f32[16,32,128]{2,1,0:T(8,128)S(1)} async-done(((f32[16,32,128]{2,1,0:T(8,128)}), f32[16,32,128]{2,1,0:T(8,128)S(1)}, u32[]{:S(2)}, u32[]{:S(2)}) %all-to-all-start.1) | async-done | bytes 262176 | tf_op jit(solution)/shard_map/prefix/all_to_all | solution.py:161
  45.7 0.5 attended.1
  46.2 13.9 %all_to_all.26.refs_0_ = f32[8,2,512]{2,1,0:T(2,128)S(1)} all-to-all(f32[8,2,512]{2,1,0:T(2,128)S(1)} %get-tuple-element.17), channel_id=1, replica_groups=mesh['seq'=16,'head'=8,'dp'=4] {'head'}, dimensions={0} | all-to-all | bytes 65536 | tf_op jit(solution)/shard_map/attended/all_to_all | solution.py:161
  60.2 1.2 %norm.1 = (bf16[512,512]{1,0:T(8,128)(2,1)}, bf16[512,512]{1,0:T(8,128)(2,1)S(1)}, f32[16,32,128]{2,1,0:T(8,128)S(1)}) custom-call(f32[8,2,512]{2,1,0:T(2,128)S(1)} %all_to_all.26.refs_0_, f32[512,512]{1,0:T(8,128)S(1)} %get-tuple-element.18.refs_1_, bf16[512,512]{1,0:T(8,128)(2,1)S(1)} %copy-done.7, f32[1,512]{1,0:T(1,128)S(1)} %bitcast.2, ...), custom_call_target="tpu_custom_call" | custom-call | flops 67108864 | bytes 3145728 | tf_op jit(solution)/shard_map/norm/pallas_call | solution.py:37
  61.4 0.8 copy-done.10
  62.2 15.2 %all_to_all.27.part_ref = f32[16,32,128]{2,1,0:T(8,128)S(1)} all-to-all(f32[16,32,128]{2,1,0:T(8,128)S(1)} %get-tuple-element.23), channel_id=1, replica_groups=mesh['seq'=16,'head'=8,'dp'=4] {'seq'}, dimensions={0} | all-to-all | bytes 524288 | tf_op jit(solution)/shard_map/suffix/all_to_all | solution.py:161
  77.3 0.7 suffix.1
  78.1 3.5 %all-to-all-start.4 = ((f32[16,32,128]{2,1,0:T(8,128)}), f32[16,32,128]{2,1,0:T(8,128)S(1)}, u32[]{:S(2)}, u32[]{:S(2)}) async-start(f32[16,32,128]{2,1,0:T(8,128)} %suffix.1), calls=%async_computation.4 | async-start | bytes 524288 | tf_op jit(solution)/shard_map/suffix/all_to_all | solution.py:161
  81.6 1.6 %copy-done.6 = bf16[4,512,512]{2,1,0:T(8,128)(2,1)S(1)} copy-done((bf16[4,512,512]{2,1,0:T(8,128)(2,1)S(1)}, bf16[4,512,512]{2,1,0:T(8,128)(2,1)}, u32[]{:S(2)}) %copy-start.6) | copy-done | bytes 2097176
  83.2 1.0 %copy-done.11 = bf16[512,512]{1,0:T(8,128)(2,1)S(1)} copy-done((bf16[512,512]{1,0:T(8,128)(2,1)S(1)}, bf16[512,512]{1,0:T(8,128)(2,1)}, u32[]{:S(2)}) %copy-start.11) | copy-done | bytes 524312
  84.2 3.1 %grad_parts.1 = (bf16[512,512]{1,0:T(8,128)(2,1)}, f32[512,512]{1,0:T(8,128)S(1)}, f32[512,512]{1,0:T(8,128)S(1)}) custom-call(bf16[512,512]{1,0:T(8,128)(2,1)S(1)} %copy-done.11, bf16[512,512]{1,0:T(8,128)(2,1)S(1)} %copy-done, bf16[512,512]{1,0:T(8,128)(2,1)S(1)} %copy-done.2, bf16[512,512]{1,0:T(8,128)(2,1)S(1)} %copy-done.4, ...), custom_call_target="tpu_custom_call" | custom-call | flops 1073741824 | bytes 5242880 | tf_op jit(solution)/shard_map/grad_parts/pallas_call | solution.py:37
  87.3 1.0 %copy-done.8 = f32[512,512]{1,0:T(8,128)} copy-done((f32[512,512]{1,0:T(8,128)}, f32[512,512]{1,0:T(8,128)S(1)}, u32[]{:S(2)}) %copy-start.8) | copy-done | bytes 1048600
  88.3 5.6 %all-to-all-done.4.refs_0_ = f32[16,32,128]{2,1,0:T(8,128)S(1)} async-done(((f32[16,32,128]{2,1,0:T(8,128)}), f32[16,32,128]{2,1,0:T(8,128)S(1)}, u32[]{:S(2)}, u32[]{:S(2)}) %all-to-all-start.4) | async-done | bytes 262176 | tf_op jit(solution)/shard_map/suffix/all_to_all | solution.py:161
  93.9 1.2 %copy-done.9 = f32[512,512]{1,0:T(8,128)S(1)} copy-done((f32[512,512]{1,0:T(8,128)S(1)}, f32[512,512]{1,0:T(8,128)}, u32[]{:S(2)}) %copy-start.9) | copy-done | bytes 1048600
  95.1 1.4 %grads.1 = (bf16[512,512]{1,0:T(8,128)(2,1)}, bf16[512,512]{1,0:T(8,128)(2,1)}) custom-call(f32[16,32,128]{2,1,0:T(8,128)S(1)} %all-to-all-done.4.refs_0_, bf16[512,512]{1,0:T(8,128)(2,1)S(1)} %copy-done.2, bf16[512,512]{1,0:T(8,128)(2,1)S(1)} %copy-done.4, f32[512,512]{1,0:T(8,128)S(1)} %get-tuple-element.24.refs_3_, f32[512,512]{1,0:T(8,128)S(1)} %copy-done.9), custom_call_target="tpu_custom_call" | custom-call | flops 134217728 | bytes 4194304 | tf_op jit(solution)/shard_map/grads/pallas_call | solution.py:37
  (17 shorter events, 0.0 us)
Async XLA Ops:
  0.6 33.0 %copy-start = (bf16[512,512]{1,0:T(8,128)(2,1)S(1)}, bf16[512,512]{1,0:T(8,128)(2,1)}, u32[]{:S(2)}) copy-start(bf16[512,512]{1,0:T(8,128)(2,1)} %refs_1_.6) | copy-start | bytes 1572868
  0.6 1.1 %copy-start.1 = (bf16[512,512]{1,0:T(8,128)(2,1)S(1)}, bf16[512,512]{1,0:T(8,128)(2,1)}, u32[]{:S(2)}) copy-start(bf16[512,512]{1,0:T(8,128)(2,1)} %refs_1_.7) | copy-start | bytes 1572868
  1.7 1.0 %copy-start.3 = (bf16[512,512]{1,0:T(8,128)(2,1)S(1)}, bf16[512,512]{1,0:T(8,128)(2,1)}, u32[]{:S(2)}) copy-start(bf16[512,512]{1,0:T(8,128)(2,1)} %refs_2_.7) | copy-start | bytes 1572868
  2.8 30.9 %copy-start.2 = (bf16[512,512]{1,0:T(8,128)(2,1)S(1)}, bf16[512,512]{1,0:T(8,128)(2,1)}, u32[]{:S(2)}) copy-start(bf16[512,512]{1,0:T(8,128)(2,1)} %refs_1_.7) | copy-start | bytes 1572868
  2.8 30.9 %copy-start.4 = (bf16[512,512]{1,0:T(8,128)(2,1)S(1)}, bf16[512,512]{1,0:T(8,128)(2,1)}, u32[]{:S(2)}) copy-start(bf16[512,512]{1,0:T(8,128)(2,1)} %refs_2_.7) | copy-start | bytes 1572868
  3.1 42.6 %copy-start.7 = (bf16[512,512]{1,0:T(8,128)(2,1)S(1)}, bf16[512,512]{1,0:T(8,128)(2,1)}, u32[]{:S(2)}) copy-start(bf16[512,512]{1,0:T(8,128)(2,1)} %refs_2_.5) | copy-start | bytes 1572868
  3.1 42.6 %copy-start.12 = (f32[512]{0:T(512)S(1)}, f32[512]{0:T(512)}, u32[]{:S(2)}) copy-start(f32[512]{0:T(512)} %param.8) | copy-start | bytes 6148
  30.1 15.6 %all-to-all-start.1 = ((f32[16,32,128]{2,1,0:T(8,128)}), f32[16,32,128]{2,1,0:T(8,128)S(1)}, u32[]{:S(2)}, u32[]{:S(2)}) async-start(f32[16,32,128]{2,1,0:T(8,128)} %prefix.1), calls=%async_computation.1 | async-start | bytes 524288 | tf_op jit(solution)/shard_map/prefix/all_to_all | solution.py:161
  35.0 1.3 %copy-start.5 = (bf16[4,512,512]{2,1,0:T(8,128)(2,1)}, bf16[4,512,512]{2,1,0:T(8,128)(2,1)S(1)}, u32[]{:S(2)}) copy-start(bf16[4,512,512]{2,1,0:T(8,128)(2,1)S(1)} %get-tuple-element.21.refs_4_) | copy-start | bytes 6291460
  61.4 0.8 copy-start.10
  78.1 15.8 %all-to-all-start.4 = ((f32[16,32,128]{2,1,0:T(8,128)}), f32[16,32,128]{2,1,0:T(8,128)S(1)}, u32[]{:S(2)}, u32[]{:S(2)}) async-start(f32[16,32,128]{2,1,0:T(8,128)} %suffix.1), calls=%async_computation.4 | async-start | bytes 524288 | tf_op jit(solution)/shard_map/suffix/all_to_all | solution.py:161
  81.6 1.6 %copy-start.6 = (bf16[4,512,512]{2,1,0:T(8,128)(2,1)S(1)}, bf16[4,512,512]{2,1,0:T(8,128)(2,1)}, u32[]{:S(2)}) copy-start(bf16[4,512,512]{2,1,0:T(8,128)(2,1)} %copy-done.5) | copy-start | bytes 6291460
  83.2 1.0 %copy-start.11 = (bf16[512,512]{1,0:T(8,128)(2,1)S(1)}, bf16[512,512]{1,0:T(8,128)(2,1)}, u32[]{:S(2)}) copy-start(bf16[512,512]{1,0:T(8,128)(2,1)} %copy-done.10) | copy-start | bytes 1572868
  87.3 1.0 %copy-start.8 = (f32[512,512]{1,0:T(8,128)}, f32[512,512]{1,0:T(8,128)S(1)}, u32[]{:S(2)}) copy-start(f32[512,512]{1,0:T(8,128)S(1)} %get-tuple-element.25.refs_4_) | copy-start | bytes 3145732
  93.9 1.2 %copy-start.9 = (f32[512,512]{1,0:T(8,128)S(1)}, f32[512,512]{1,0:T(8,128)}, u32[]{:S(2)}) copy-start(f32[512,512]{1,0:T(8,128)} %copy-done.8) | copy-start | bytes 3145732

commit v2 on v1

v2 whole, which is shorter than its diff:
```python
import jax
import jax.numpy as jnp
from jax import lax
from jax.experimental import pallas as pl
from jax.experimental.pallas import tpu as pltpu
from jax.sharding import PartitionSpec as P

HD = 128
FEAT = 4096
EPS = 1e-06
F32 = jnp.float32
BF16 = jnp.bfloat16
VMEM_LIMIT = 24 * 1024 * 1024


def dot(a, b, contract):
    return lax.dot_general(a, b, ((contract[0], contract[1]), ((), ())), preferred_element_type=F32)


def nn(a, b):
    return dot(a, b, ((1,), (0,)))


def nt(a, b):
    return dot(a, b, ((1,), (1,)))


def tn(a, b):
    return dot(a, b, ((0,), (0,)))


def head_columns(h):
    return slice(h * HD, (h + 1) * HD)


def call(kernel, out_shape, *operands, **extra):
    return pl.pallas_call(
        kernel,
        out_shape=out_shape,
        compiler_params=pltpu.CompilerParams(vmem_limit_bytes=VMEM_LIMIT),
        **extra,
    )(*operands)


def shape_of(shape, dtype=F32):
    return jax.ShapeDtypeStruct(shape, dtype)


def state_of_heads(ref, heads):
    return ref[...].reshape(heads, HD, HD).astype(BF16)


def store_state(state_ref, heads, h, state):
    per_head = state_ref.shape[0] // heads
    state_ref[h * per_head : (h + 1) * per_head] = state.reshape(per_head, state_ref.shape[1], HD)


def outer_kernel(heads, a_hbm, b_hbm, state_ref, a_ref, b_ref, sems):
    copies = []
    parts = halves(a_ref.shape[0])
    for j, rows in enumerate(parts):
        pair = []
        for i, (source, target) in enumerate(((a_hbm, a_ref), (b_hbm, b_ref))):
            copy = pltpu.make_async_copy(source.at[rows], target.at[rows], sems.at[j, i])
            copy.start()
            pair.append(copy)
        copies.append(pair)
    states = [None] * heads
    for j, rows in enumerate(parts):
        for copy in copies[j]:
            copy.wait()
        for h in range(heads):
            cols = head_columns(h)
            state = tn(a_ref[rows, cols], b_ref[rows, cols])
            states[h] = state if j == 0 else states[h] + state
    for h in range(heads):
        store_state(state_ref, heads, h, states[h])


def prefix_kernel(part_ref, out_ref):
    n = part_ref.shape[0]
    total = jnp.zeros(part_ref.shape[1:], F32)
    for m in range(n):
        out_ref[m] = total
        if m < n - 1:
            total = total + part_ref[m]


def suffix_kernel(part_ref, out_ref):
    n = part_ref.shape[0]
    total = jnp.zeros(part_ref.shape[1:], F32)
    for m in reversed(range(n)):
        out_ref[m] = total
        if m > 0:
            total = total + part_ref[m]


def causal_mask(rows):
    t = lax.broadcasted_iota(jnp.int32, (rows, rows), 0)
    s = lax.broadcasted_iota(jnp.int32, (rows, rows), 1)
    return t >= s


def cut(block, mask):
    return jnp.where(mask, block, 0.0).astype(BF16)


def halves(tokens):
    return slice(0, tokens // 2), slice(tokens // 2, tokens)


def attend_kernel(heads, q_ref, k_ref, v_ref, p_ref, c_ref, g_ref, a_ref, w_ref, sums_ref):
    tokens = q_ref.shape[0]
    state = state_of_heads(p_ref, heads)
    mask = causal_mask(tokens // 2)
    first, second = halves(tokens)
    squares = [jnp.zeros((tokens // 2, HD), F32)] * 2
    inner = [jnp.zeros((tokens // 2, HD), F32)] * 2
    for h in range(heads):
        cols = head_columns(h)
        q0, q1 = q_ref[first, cols], q_ref[second, cols]
        k0, k1 = k_ref[first, cols], k_ref[second, cols]
        v0, v1 = v_ref[first, cols], v_ref[second, cols]
        w00 = cut(nt(q0, k0), mask)
        w10 = nt(q1, k0).astype(BF16)
        w11 = cut(nt(q1, k1), mask)
        w_ref[h, 0] = w00
        w_ref[h, 1] = w10
        w_ref[h, 2] = w11
        attended = (
            nn(q0, state[h]) + nn(w00, v0),
            nn(q1, state[h]) + (nn(w10, v0) + nn(w11, v1)),
        )
        for i, rows in enumerate((first, second)):
            a_ref[rows, cols] = attended[i]
            scaled = c_ref[rows, cols].astype(F32) * g_ref[:, cols]
            squares[i] = squares[i] + attended[i] * attended[i]
            inner[i] = inner[i] + scaled * attended[i]
    squares = jnp.concatenate([jnp.sum(part.T, axis=0, keepdims=True) for part in squares], axis=1)
    inner = jnp.concatenate([jnp.sum(part.T, axis=0, keepdims=True) for part in inner], axis=1)
    both = jnp.concatenate([squares, inner], axis=0)
    for i in range(sums_ref.shape[0]):
        sums_ref[i] = both


def norm_columns(s_ref):
    sums = s_ref[0]
    for i in range(1, s_ref.shape[0]):
        sums = sums + s_ref[i]
    inverse = lax.rsqrt(sums[0:1] / FEAT + EPS)
    slope = sums[1:2] * inverse * inverse / FEAT
    tokens = sums.shape[1]
    rows = jnp.concatenate(
        [jnp.broadcast_to(inverse, (64, tokens)), jnp.broadcast_to(slope, (64, tokens))], axis=0
    ).T
    return rows[:, 0:1], rows[:, 64:65]


def norm_kernel(heads, s_ref, a_ref, c_ref, g_ref, q_ref, d_ref, state_ref):
    inverse, slope = norm_columns(s_ref)
    for h in range(heads):
        cols = head_columns(h)
        scaled = c_ref[:, cols].astype(F32) * g_ref[:, cols]
        grad = (inverse * (scaled - a_ref[:, cols] * slope)).astype(BF16)
        d_ref[:, cols] = grad
        store_state(state_ref, heads, h, tn(q_ref[:, cols], grad))


def grad_kernel(
    heads, r_ref, s_ref, a_ref, g_ref, d_ref, q_ref, k_ref, v_ref, w_ref, p_ref,
    o_hbm, gq_hbm, gk_hbm, gv_hbm, o_ref, gq_ref, gk_ref, gv_ref, sems,
):
    copies = []

    def send(i, h, source, target):
        cols = head_columns(h)
        copy = pltpu.make_async_copy(source.at[:, cols], target.at[:, cols], sems.at[i, h])
        copy.start()
        copies.append(copy)

    tokens = q_ref.shape[0]
    first, second = halves(tokens)
    mask = causal_mask(tokens // 2)
    inverse, _ = norm_columns(s_ref)
    for h in range(heads):
        cols = head_columns(h)
        o_ref[:, cols] = (a_ref[:, cols] * inverse * g_ref[:, cols]).astype(BF16)
        send(0, h, o_ref, o_hbm)
    prefix = state_of_heads(p_ref, heads)
    suffix = state_of_heads(r_ref, heads)
    for h in range(heads):
        cols = head_columns(h)
        q0, q1 = q_ref[first, cols], q_ref[second, cols]
        k0, k1 = k_ref[first, cols], k_ref[second, cols]
        v0, v1 = v_ref[first, cols], v_ref[second, cols]
        d0, d1 = d_ref[first, cols], d_ref[second, cols]
        g00 = cut(nt(d0, v0), mask)
        g10 = nt(d1, v0).astype(BF16)
        g11 = cut(nt(d1, v1), mask)
        gq_ref[first, cols] = (nt(d0, prefix[h]) + nn(g00, k0)).astype(BF16)
        gq_ref[second, cols] = (nt(d1, prefix[h]) + (nn(g10, k0) + nn(g11, k1))).astype(BF16)
        send(1, h, gq_ref, gq_hbm)
        gk_ref[first, cols] = (nt(v0, suffix[h]) + (tn(g00, q0) + tn(g10, q1))).astype(BF16)
        gk_ref[second, cols] = (nt(v1, suffix[h]) + tn(g11, q1)).astype(BF16)
        send(2, h, gk_ref, gk_hbm)
        w00, w10, w11 = w_ref[h, 0], w_ref[h, 1], w_ref[h, 2]
        gv_ref[first, cols] = (nn(k0, suffix[h]) + (tn(w00, d0) + tn(w10, d1))).astype(BF16)
        gv_ref[second, cols] = (nn(k1, suffix[h]) + tn(w11, d1)).astype(BF16)
        send(3, h, gv_ref, gv_hbm)
    for copy in copies:
        copy.wait()


def exchange(parts, axis):
    return lax.all_to_all(parts, axis, 0, 0, tiled=True)


def per_device(queries, key_vectors, value_vectors, norm_gain, cotangent):
    tokens, features = queries.shape
    heads = features // HD
    seq = lax.axis_size("seq")
    head_devices = lax.axis_size("head")
    state_shape = (seq, heads * HD // seq, HD)
    wide = (tokens, features)
    gain = norm_gain.reshape(1, features)

    def bind(kernel):
        return lambda *refs: kernel(heads, *refs)

    in_hbm = pl.BlockSpec(memory_space=pltpu.HBM)
    in_vmem = pl.BlockSpec(memory_space=pltpu.VMEM)

    with jax.named_scope("key_value_state"):
        local_kv = call(
            bind(outer_kernel),
            shape_of(state_shape),
            pltpu.with_memory_space_constraint(key_vectors, pltpu.HBM),
            pltpu.with_memory_space_constraint(value_vectors, pltpu.HBM),
            in_specs=[in_hbm, in_hbm],
            out_specs=in_vmem,
            scratch_shapes=[
                pltpu.VMEM(wide, BF16),
                pltpu.VMEM(wide, BF16),
                pltpu.SemaphoreType.DMA((heads, 2)),
            ],
        )
    with jax.named_scope("prefix"):
        pieces = exchange(local_kv, "seq")
        sums = call(prefix_kernel, shape_of(state_shape), pieces)
        prefix = exchange(sums, "seq")
    with jax.named_scope("attended"):
        attended, weights, sums = call(
            bind(attend_kernel),
            (
                shape_of(wide),
                shape_of((heads, 3, tokens // 2, tokens // 2), BF16),
                shape_of((head_devices, 2, tokens)),
            ),
            queries,
            key_vectors,
            value_vectors,
            prefix,
            cotangent,
            gain,
        )
        sums = exchange(sums, "head")
    with jax.named_scope("norm"):
        out_grad, local_qg = call(
            bind(norm_kernel),
            (shape_of(wide, BF16), shape_of(state_shape)),
            sums,
            attended,
            cotangent,
            gain,
            queries,
        )
    with jax.named_scope("suffix"):
        pieces = exchange(local_qg, "seq")
        totals = call(suffix_kernel, shape_of(state_shape), pieces)
        suffix = exchange(totals, "seq")
    with jax.named_scope("grads"):
        return call(
            bind(grad_kernel),
            (shape_of(wide, BF16),) * 4,
            suffix,
            sums,
            attended,
            gain,
            out_grad,
            queries,
            key_vectors,
            value_vectors,
            weights,
            prefix,
            in_specs=[in_vmem] * 10,
            out_specs=[in_hbm] * 4,
            scratch_shapes=[pltpu.VMEM(wide, BF16)] * 4 + [pltpu.SemaphoreType.DMA((4, heads))],
        )


def solution(mesh):
    split = P(("dp", "seq"), "head")
    return jax.shard_map(
        per_device,
        mesh=mesh,
        in_specs=(split, split, split, P("head"), split),
        out_specs=(split, split, split, split),
        check_vma=False,
    )
```

time: 97.1 us -> 94.7 us (0.975)
  the two profiles are of different devices: /device:TPU:8 before, /device:TPU:64 now
where the time goes in v2:
time: 94.7 us; the launch traced here: 94.2 us
  blocking collectives  85.8 us (91%)
  Pallas kernels  7.59 us (8%)
    all_to_all x5, blocking collectives, exchange(): return lax.all_to_all(parts, axis, 0, 0, tiled=True)  85.8 us
    pallas_call x6, Pallas kernels, call(): pl.pallas_call(kernel, out_shape=out_shape, compiler_params=pltpu.Compile...  7.59 us

profile of v2, /device:TPU:64, one launch (start us, length us, event | category | flops | bytes accessed | tf_op | source)
XLA Modules:
  0.0 94.2 jit_solution(3297766239724020315)
XLA Ops:
  0.6 0.0 copy-start.2
  0.6 0.0 copy-start.1
  0.7 0.0 copy-start
  0.7 0.0 copy-start.3
  0.7 0.0 copy-start.4
  0.7 1.7 %key_value_state.1 = f32[16,32,128]{2,1,0:T(8,128)S(1)} custom-call(bf16[512,512]{1,0:T(8,128)(2,1)} %refs_6_.1, bf16[512,512]{1,0:T(8,128)(2,1)} %refs_7_.1), custom_call_target="tpu_custom_call" | custom-call | tf_op jit(solution)/shard_map/key_value_state/pallas_call | solution.py:37
  2.4 25.0 %all_to_all.25.part_ref = f32[16,32,128]{2,1,0:T(8,128)S(1)} all-to-all(f32[16,32,128]{2,1,0:T(8,128)S(1)} %key_value_state.1), channel_id=1, replica_groups=mesh['seq'=16,'head'=8,'dp'=4] {'seq'}, dimensions={0} | all-to-all | bytes 524288 | tf_op jit(solution)/shard_map/prefix/all_to_all | solution.py:215
  27.4 16.4 %all_to_all.26.refs_3_.refs_9_ = f32[16,32,128]{2,1,0:T(8,128)S(1)} all-to-all(f32[16,32,128]{2,1,0:T(8,128)S(1)} %prefix.1), channel_id=1, replica_groups=mesh['seq'=16,'head'=8,'dp'=4] {'seq'}, dimensions={0} | all-to-all | bytes 524288 | tf_op jit(solution)/shard_map/prefix/all_to_all | solution.py:215
  43.8 0.0 copy-done.2
  43.8 0.0 copy-done.1
  43.8 0.0 copy-done
  43.8 0.0 copy-done.3
  43.9 0.0 copy-done.4
  43.9 1.4 %attended.1 = (f32[512,512]{1,0:T(8,128)S(1)}, bf16[4,3,256,256]{3,2,1,0:T(8,128)(2,1)S(1)}, f32[8,2,512]{2,1,0:T(2,128)S(1)}) custom-call(bf16[512,512]{1,0:T(8,128)(2,1)S(1)} %copy-done, bf16[512,512]{1,0:T(8,128)(2,1)S(1)} %copy-done.1, bf16[512,512]{1,0:T(8,128)(2,1)S(1)} %copy-done.2, f32[16,32,128]{2,1,0:T(8,128)S(1)} %all_to_all.26.refs_3_.refs_9_, ...), custom_call_target="tpu_custom_call" | custom-call | tf_op jit(solution)/shard_map/attended/pallas_call | solution.py:37
  45.2 14.9 %all_to_all.27.refs_0_.refs_1_ = f32[8,2,512]{2,1,0:T(2,128)S(1)} all-to-all(f32[8,2,512]{2,1,0:T(2,128)S(1)} %get-tuple-element.9), channel_id=1, replica_groups=mesh['seq'=16,'head'=8,'dp'=4] {'head'}, dimensions={0} | all-to-all | bytes 65536 | tf_op jit(solution)/shard_map/attended/all_to_all | solution.py:215
  60.2 0.7 norm.1
  60.9 14.4 %all_to_all.28.part_ref = f32[16,32,128]{2,1,0:T(8,128)S(1)} all-to-all(f32[16,32,128]{2,1,0:T(8,128)S(1)} %get-tuple-element.11), channel_id=1, replica_groups=mesh['seq'=16,'head'=8,'dp'=4] {'seq'}, dimensions={0} | all-to-all | bytes 524288 | tf_op jit(solution)/shard_map/suffix/all_to_all | solution.py:215
  75.3 15.1 %all_to_all.29.refs_0_ = f32[16,32,128]{2,1,0:T(8,128)S(1)} all-to-all(f32[16,32,128]{2,1,0:T(8,128)S(1)} %suffix.1), channel_id=1, replica_groups=mesh['seq'=16,'head'=8,'dp'=4] {'seq'}, dimensions={0} | all-to-all | bytes 524288 | tf_op jit(solution)/shard_map/suffix/all_to_all | solution.py:215
  90.4 3.7 %grads.1 = (bf16[512,512]{1,0:T(8,128)(2,1)}, bf16[512,512]{1,0:T(8,128)(2,1)}, bf16[512,512]{1,0:T(8,128)(2,1)}, bf16[512,512]{1,0:T(8,128)(2,1)}) custom-call(f32[16,32,128]{2,1,0:T(8,128)S(1)} %all_to_all.29.refs_0_, f32[8,2,512]{2,1,0:T(2,128)S(1)} %all_to_all.27.refs_0_.refs_1_, f32[512,512]{1,0:T(8,128)S(1)} %get-tuple-element.10.refs_1_.refs_2_, ...), custom_call_target="tpu_custom_call" | custom-call | tf_op jit(solution)/shard_map/grads/pallas_call | solution.py:37
  (2 shorter events, 0.0 us)
Async XLA Ops:
  0.6 43.2 %copy-start.2 = (bf16[512,512]{1,0:T(8,128)(2,1)S(1)}, bf16[512,512]{1,0:T(8,128)(2,1)}, u32[]{:S(2)}) copy-start(bf16[512,512]{1,0:T(8,128)(2,1)} %refs_7_.1) | copy-start | bytes 1572868
  0.6 43.2 %copy-start.1 = (bf16[512,512]{1,0:T(8,128)(2,1)S(1)}, bf16[512,512]{1,0:T(8,128)(2,1)}, u32[]{:S(2)}) copy-start(bf16[512,512]{1,0:T(8,128)(2,1)} %refs_6_.1) | copy-start | bytes 1572868
  0.7 43.2 %copy-start = (bf16[512,512]{1,0:T(8,128)(2,1)S(1)}, bf16[512,512]{1,0:T(8,128)(2,1)}, u32[]{:S(2)}) copy-start(bf16[512,512]{1,0:T(8,128)(2,1)} %refs_5_.1) | copy-start | bytes 1572868
  0.7 43.2 %copy-start.3 = (bf16[512,512]{1,0:T(8,128)(2,1)S(1)}, bf16[512,512]{1,0:T(8,128)(2,1)}, u32[]{:S(2)}) copy-start(bf16[512,512]{1,0:T(8,128)(2,1)} %refs_2_.3) | copy-start | bytes 1572868
  0.7 43.2 %copy-start.4 = (f32[512]{0:T(512)S(1)}, f32[512]{0:T(512)}, u32[]{:S(2)}) copy-start(f32[512]{0:T(512)} %param.8) | copy-start | bytes 6148

commit v3 on v2

--- a/solution.py
+++ b/solution.py
@@ -120,22 +120,30 @@
         cols = head_columns(h)
         q0, q1 = q_ref[first, cols], q_ref[second, cols]
         k0, k1 = k_ref[first, cols], k_ref[second, cols]
-        v0, v1 = v_ref[first, cols], v_ref[second, cols]
         w00 = cut(nt(q0, k0), mask)
         w10 = nt(q1, k0).astype(BF16)
         w11 = cut(nt(q1, k1), mask)
         w_ref[h, 0] = w00
         w_ref[h, 1] = w10
         w_ref[h, 2] = w11
+    for h in range(heads):
+        cols = head_columns(h)
+        q0, q1 = q_ref[first, cols], q_ref[second, cols]
+        v0, v1 = v_ref[first, cols], v_ref[second, cols]
+        w00, w10, w11 = w_ref[h, 0], w_ref[h, 1], w_ref[h, 2]
         attended = (
             nn(q0, state[h]) + nn(w00, v0),
             nn(q1, state[h]) + (nn(w10, v0) + nn(w11, v1)),
         )
         for i, rows in enumerate((first, second)):
             a_ref[rows, cols] = attended[i]
+    for h in range(heads):
+        cols = head_columns(h)
+        for i, rows in enumerate((first, second)):
+            part = a_ref[rows, cols]
             scaled = c_ref[rows, cols].astype(F32) * g_ref[:, cols]
-            squares[i] = squares[i] + attended[i] * attended[i]
-            inner[i] = inner[i] + scaled * attended[i]
+            squares[i] = squares[i] + part * part
+            inner[i] = inner[i] + scaled * part
     squares = jnp.concatenate([jnp.sum(part.T, axis=0, keepdims=True) for part in squares], axis=1)
     inner = jnp.concatenate([jnp.sum(part.T, axis=0, keepdims=True) for part in inner], axis=1)
     both = jnp.concatenate([squares, inner], axis=0)
@@ -156,7 +164,7 @@
     return rows[:, 0:1], rows[:, 64:65]
 
 
-def norm_kernel(heads, s_ref, a_ref, c_ref, g_ref, q_ref, d_ref, state_ref):
+def norm_kernel(heads, s_ref, a_ref, c_ref, g_ref, q_ref, d_ref, state_ref, o_ref):
     inverse, slope = norm_columns(s_ref)
     for h in range(heads):
         cols = head_columns(h)
@@ -164,11 +172,12 @@
         grad = (inverse * (scaled - a_ref[:, cols] * slope)).astype(BF16)
         d_ref[:, cols] = grad
         store_state(state_ref, heads, h, tn(q_ref[:, cols], grad))
+        o_ref[:, cols] = (a_ref[:, cols] * inverse * g_ref[:, cols]).astype(BF16)
 
 
 def grad_kernel(
-    heads, r_ref, s_ref, a_ref, g_ref, d_ref, q_ref, k_ref, v_ref, w_ref, p_ref,
-    o_hbm, gq_hbm, gk_hbm, gv_hbm, o_ref, gq_ref, gk_ref, gv_ref, sems,
+    heads, r_ref, d_ref, q_ref, k_ref, v_ref, w_ref, p_ref, o_ref,
+    o_hbm, gq_hbm, gk_hbm, gv_hbm, gq_ref, gk_ref, gv_ref, gw_ref, sems,
 ):
     copies = []
 
@@ -178,25 +187,27 @@
         copy.start()
         copies.append(copy)
 
+    for h in range(heads):
+        send(0, h, o_ref, o_hbm)
     tokens = q_ref.shape[0]
     first, second = halves(tokens)
     mask = causal_mask(tokens // 2)
-    inverse, _ = norm_columns(s_ref)
-    for h in range(heads):
-        cols = head_columns(h)
-        o_ref[:, cols] = (a_ref[:, cols] * inverse * g_ref[:, cols]).astype(BF16)
-        send(0, h, o_ref, o_hbm)
     prefix = state_of_heads(p_ref, heads)
     suffix = state_of_heads(r_ref, heads)
+    for h in range(heads):
+        cols = head_columns(h)
+        v0, v1 = v_ref[first, cols], v_ref[second, cols]
+        d0, d1 = d_ref[first, cols], d_ref[second, cols]
+        gw_ref[h, 0] = cut(nt(d0, v0), mask)
+        gw_ref[h, 1] = nt(d1, v0).astype(BF16)
+        gw_ref[h, 2] = cut(nt(d1, v1), mask)
     for h in range(heads):
         cols = head_columns(h)
         q0, q1 = q_ref[first, cols], q_ref[second, cols]
         k0, k1 = k_ref[first, cols], k_ref[second, cols]
         v0, v1 = v_ref[first, cols], v_ref[second, cols]
         d0, d1 = d_ref[first, cols], d_ref[second, cols]
-        g00 = cut(nt(d0, v0), mask)
-        g10 = nt(d1, v0).astype(BF16)
-        g11 = cut(nt(d1, v1), mask)
+        g00, g10, g11 = gw_ref[h, 0], gw_ref[h, 1], gw_ref[h, 2]
         gq_ref[first, cols] = (nt(d0, prefix[h]) + nn(g00, k0)).astype(BF16)
         gq_ref[second, cols] = (nt(d1, prefix[h]) + (nn(g10, k0) + nn(g11, k1))).astype(BF16)
         send(1, h, gq_ref, gq_hbm)
@@ -265,9 +276,9 @@
         )
         sums = exchange(sums, "head")
     with jax.named_scope("norm"):
-        out_grad, local_qg = call(
+        out_grad, local_qg, layer_out = call(
             bind(norm_kernel),
-            (shape_of(wide, BF16), shape_of(state_shape)),
+            (shape_of(wide, BF16), shape_of(state_shape), shape_of(wide, BF16)),
             sums,
             attended,
             cotangent,
@@ -283,18 +294,16 @@
             bind(grad_kernel),
             (shape_of(wide, BF16),) * 4,
             suffix,
-            sums,
-            attended,
-            gain,
             out_grad,
             queries,
             key_vectors,
             value_vectors,
             weights,
             prefix,
-            in_specs=[in_vmem] * 10,
+            layer_out,
+            in_specs=[in_vmem] * 8,
             out_specs=[in_hbm] * 4,
-            scratch_shapes=[pltpu.VMEM(wide, BF16)] * 4 + [pltpu.SemaphoreType.DMA((4, heads))],
+            scratch_shapes=[pltpu.VMEM(wide, BF16)] * 3 + [pltpu.VMEM((heads, 3, tokens // 2, tokens // 2), BF16), pltpu.SemaphoreType.DMA((4, heads))],
         )
 
 

time: 94.7 us -> 94.1 us (level)
  the two profiles are of different devices: /device:TPU:64 before, /device:TPU:8 now
where the time goes in v3:
time: 94.1 us; the launch traced here: 93.8 us
  blocking collectives  86.1 us (91%)
  Pallas kernels  7.02 us (7%)
    all_to_all x5, blocking collectives, exchange(): return lax.all_to_all(parts, axis, 0, 0, tiled=True)  86.1 us
    pallas_call x6, Pallas kernels, call(): pl.pallas_call(kernel, out_shape=out_shape, compiler_params=pltpu.Compile...  7.02 us

profile of v3, /device:TPU:8, one launch (start us, length us, event | category | flops | bytes accessed | tf_op | source)
XLA Modules:
  0.0 93.8 jit_solution(1118297547290276974)
XLA Ops:
  0.6 0.0 copy-start.2
  0.6 0.0 copy-start.1
  0.7 0.0 copy-start
  0.7 0.0 copy-start.3
  0.7 0.0 copy-start.4
  0.7 1.7 %key_value_state.1 = f32[16,32,128]{2,1,0:T(8,128)S(1)} custom-call(bf16[512,512]{1,0:T(8,128)(2,1)} %refs_3_.1, bf16[512,512]{1,0:T(8,128)(2,1)} %refs_4_.5), custom_call_target="tpu_custom_call" | custom-call | tf_op jit(solution)/shard_map/key_value_state/pallas_call | solution.py:37
  2.4 26.1 %all_to_all.25.part_ref = f32[16,32,128]{2,1,0:T(8,128)S(1)} all-to-all(f32[16,32,128]{2,1,0:T(8,128)S(1)} %key_value_state.1), channel_id=1, replica_groups=mesh['seq'=16,'head'=8,'dp'=4] {'seq'}, dimensions={0} | all-to-all | bytes 524288 | tf_op jit(solution)/shard_map/prefix/all_to_all | solution.py:226
  28.6 14.7 %all_to_all.26.refs_3_.refs_6_ = f32[16,32,128]{2,1,0:T(8,128)S(1)} all-to-all(f32[16,32,128]{2,1,0:T(8,128)S(1)} %prefix.1), channel_id=1, replica_groups=mesh['seq'=16,'head'=8,'dp'=4] {'seq'}, dimensions={0} | all-to-all | bytes 524288 | tf_op jit(solution)/shard_map/prefix/all_to_all | solution.py:226
  43.3 0.0 copy-done.2
  43.3 0.0 copy-done.1
  43.3 0.0 copy-done
  43.3 0.0 copy-done.3
  43.3 0.0 copy-done.4
  43.3 1.4 %attended.1 = (f32[512,512]{1,0:T(8,128)S(1)}, bf16[4,3,256,256]{3,2,1,0:T(8,128)(2,1)S(1)}, f32[8,2,512]{2,1,0:T(2,128)S(1)}) custom-call(bf16[512,512]{1,0:T(8,128)(2,1)S(1)} %copy-done, bf16[512,512]{1,0:T(8,128)(2,1)S(1)} %copy-done.1, bf16[512,512]{1,0:T(8,128)(2,1)S(1)} %copy-done.2, f32[16,32,128]{2,1,0:T(8,128)S(1)} %all_to_all.26.refs_3_.refs_6_, ...), custom_call_target="tpu_custom_call" | custom-call | tf_op jit(solution)/shard_map/attended/pallas_call | solution.py:37
  44.7 13.9 %all_to_all.27.refs_0_ = f32[8,2,512]{2,1,0:T(2,128)S(1)} all-to-all(f32[8,2,512]{2,1,0:T(2,128)S(1)} %get-tuple-element.10), channel_id=1, replica_groups=mesh['seq'=16,'head'=8,'dp'=4] {'head'}, dimensions={0} | all-to-all | bytes 65536 | tf_op jit(solution)/shard_map/attended/all_to_all | solution.py:226
  58.6 0.8 norm.1
  59.4 16.4 %all_to_all.28.part_ref = f32[16,32,128]{2,1,0:T(8,128)S(1)} all-to-all(f32[16,32,128]{2,1,0:T(8,128)S(1)} %get-tuple-element.12), channel_id=1, replica_groups=mesh['seq'=16,'head'=8,'dp'=4] {'seq'}, dimensions={0} | all-to-all | bytes 524288 | tf_op jit(solution)/shard_map/suffix/all_to_all | solution.py:226
  75.8 15.0 %all_to_all.29.refs_0_ = f32[16,32,128]{2,1,0:T(8,128)S(1)} all-to-all(f32[16,32,128]{2,1,0:T(8,128)S(1)} %suffix.1), channel_id=1, replica_groups=mesh['seq'=16,'head'=8,'dp'=4] {'seq'}, dimensions={0} | all-to-all | bytes 524288 | tf_op jit(solution)/shard_map/suffix/all_to_all | solution.py:226
  90.7 3.1 %grads.1 = (bf16[512,512]{1,0:T(8,128)(2,1)}, bf16[512,512]{1,0:T(8,128)(2,1)}, bf16[512,512]{1,0:T(8,128)(2,1)}, bf16[512,512]{1,0:T(8,128)(2,1)}) custom-call(f32[16,32,128]{2,1,0:T(8,128)S(1)} %all_to_all.29.refs_0_, bf16[512,512]{1,0:T(8,128)(2,1)S(1)} %get-tuple-element.13.refs_1_, bf16[512,512]{1,0:T(8,128)(2,1)S(1)} %copy-done, ...), custom_call_target="tpu_custom_call" | custom-call | tf_op jit(solution)/shard_map/grads/pallas_call | solution.py:37
  (2 shorter events, 0.0 us)
Async XLA Ops:
  0.6 42.7 %copy-start.2 = (bf16[512,512]{1,0:T(8,128)(2,1)S(1)}, bf16[512,512]{1,0:T(8,128)(2,1)}, u32[]{:S(2)}) copy-start(bf16[512,512]{1,0:T(8,128)(2,1)} %refs_4_.5) | copy-start | bytes 1572868
  0.6 42.7 %copy-start.1 = (bf16[512,512]{1,0:T(8,128)(2,1)S(1)}, bf16[512,512]{1,0:T(8,128)(2,1)}, u32[]{:S(2)}) copy-start(bf16[512,512]{1,0:T(8,128)(2,1)} %refs_3_.1) | copy-start | bytes 1572868
  0.7 42.7 %copy-start = (bf16[512,512]{1,0:T(8,128)(2,1)S(1)}, bf16[512,512]{1,0:T(8,128)(2,1)}, u32[]{:S(2)}) copy-start(bf16[512,512]{1,0:T(8,128)(2,1)} %refs_2_.5) | copy-start | bytes 1572868
  0.7 42.7 %copy-start.3 = (bf16[512,512]{1,0:T(8,128)(2,1)S(1)}, bf16[512,512]{1,0:T(8,128)(2,1)}, u32[]{:S(2)}) copy-start(bf16[512,512]{1,0:T(8,128)(2,1)} %refs_2_.4) | copy-start | bytes 1572868
  0.7 42.7 %copy-start.4 = (f32[512]{0:T(512)S(1)}, f32[512]{0:T(512)}, u32[]{:S(2)}) copy-start(f32[512]{0:T(512)} %param.8) | copy-start | bytes 6148

commit v4 on v3

--- a/solution.py
+++ b/solution.py
@@ -1,3 +1,5 @@
+import functools
+
 import jax
 import jax.numpy as jnp
 from jax import lax
@@ -10,7 +12,14 @@
 EPS = 1e-06
 F32 = jnp.float32
 BF16 = jnp.bfloat16
+FORWARD_FIRST = 11
+BACKWARD_FIRST = 11
+HEAD_FIRST = 4
 VMEM_LIMIT = 24 * 1024 * 1024
+
+
+def rotated(n, first):
+    return [(first + i) % n for i in range(n)]
 
 
 def dot(a, b, contract):
@@ -77,22 +86,12 @@
         store_state(state_ref, heads, h, states[h])
 
 
-def prefix_kernel(part_ref, out_ref):
-    n = part_ref.shape[0]
+def scan_kernel(slots, part_ref, out_ref):
     total = jnp.zeros(part_ref.shape[1:], F32)
-    for m in range(n):
-        out_ref[m] = total
-        if m < n - 1:
-            total = total + part_ref[m]
-
-
-def suffix_kernel(part_ref, out_ref):
-    n = part_ref.shape[0]
-    total = jnp.zeros(part_ref.shape[1:], F32)
-    for m in reversed(range(n)):
-        out_ref[m] = total
-        if m > 0:
-            total = total + part_ref[m]
+    for slot in slots:
+        out_ref[slot] = total
+        if slot != slots[-1]:
+            total = total + part_ref[slot]
 
 
 def causal_mask(rows):
@@ -222,8 +221,14 @@
         copy.wait()
 
 
-def exchange(parts, axis):
-    return lax.all_to_all(parts, axis, 0, 0, tiled=True)
+def exchange(parts, axis, order):
+    return lax.all_to_all(parts, axis, 0, 0, tiled=True, axis_index_groups=[order])
+
+
+def exclusive_scan(local, slots, order):
+    pieces = exchange(local, "seq", order)
+    sums = call(functools.partial(scan_kernel, slots), shape_of(local.shape), pieces)
+    return exchange(sums, "seq", order)
 
 
 def per_device(queries, key_vectors, value_vectors, norm_gain, cotangent):
@@ -256,9 +261,8 @@
             ],
         )
     with jax.named_scope("prefix"):
-        pieces = exchange(local_kv, "seq")
-        sums = call(prefix_kernel, shape_of(state_shape), pieces)
-        prefix = exchange(sums, "seq")
+        order = rotated(seq, FORWARD_FIRST)
+        prefix = exclusive_scan(local_kv, [order.index(m) for m in range(seq)], order)
     with jax.named_scope("attended"):
         attended, weights, sums = call(
             bind(attend_kernel),
@@ -274,7 +278,7 @@
             cotangent,
             gain,
         )
-        sums = exchange(sums, "head")
+        sums = exchange(sums, "head", rotated(head_devices, HEAD_FIRST))
     with jax.named_scope("norm"):
         out_grad, local_qg, layer_out = call(
             bind(norm_kernel),
@@ -286,9 +290,8 @@
             queries,
         )
     with jax.named_scope("suffix"):
-        pieces = exchange(local_qg, "seq")
-        totals = call(suffix_kernel, shape_of(state_shape), pieces)
-        suffix = exchange(totals, "seq")
+        order = rotated(seq, BACKWARD_FIRST)
+        suffix = exclusive_scan(local_qg, [order.index(m) for m in reversed(range(seq))], order)
     with jax.named_scope("grads"):
         return call(
             bind(grad_kernel),

time: 94.1 us -> 84.3 us (0.90)
  the two profiles are of different devices: /device:TPU:8 before, /device:TPU:64 now
where the time goes in v4:
time: 84.3 us; the launch traced here: 84 us
  blocking collectives  76.2 us (90%)
  Pallas kernels  7.03 us (8%)
    all_to_all x5, blocking collectives, exchange(): lax.all_to_all(parts, axis, 0, 0, tiled=True, axis_index_groups=[order])  76.2 us
    pallas_call x6, Pallas kernels, call(): pl.pallas_call(kernel, out_shape=out_shape, compiler_params=pltpu.Compile...  7.03 us

profile of v4, /device:TPU:64, one launch (start us, length us, event | category | flops | bytes accessed | tf_op | source)
XLA Modules:
  0.0 84.0 jit_solution(18101851289065427824)
XLA Ops:
  0.6 0.0 copy-start.2
  0.6 0.0 copy-start.1
  0.7 0.0 copy-start
  0.7 0.0 copy-start.3
  0.7 0.0 copy-start.4
  0.7 1.7 %key_value_state.1 = f32[16,32,128]{2,1,0:T(8,128)S(1)} custom-call(bf16[512,512]{1,0:T(8,128)(2,1)} %refs_3_.1, bf16[512,512]{1,0:T(8,128)(2,1)} %refs_4_.5), custom_call_target="tpu_custom_call" | custom-call | tf_op jit(solution)/shard_map/key_value_state/pallas_call | solution.py:46
  2.4 20.9 %all_to_all.25.part_ref = f32[16,32,128]{2,1,0:T(8,128)S(1)} all-to-all(f32[16,32,128]{2,1,0:T(8,128)S(1)} %key_value_state.1), channel_id=1, replica_groups={{352,384,416,448,480,0,32,64,96,128,160,192,224,256,288,320},{353,385,4..., dimensions={0} | all-to-all | bytes 524288 | tf_op jit(solution)/shard_map/prefix/all_to_all | solution.py:225
  23.4 15.9 %all_to_all.26.refs_3_.refs_6_ = f32[16,32,128]{2,1,0:T(8,128)S(1)} all-to-all(f32[16,32,128]{2,1,0:T(8,128)S(1)} %prefix.1), channel_id=1, replica_groups={{352,384,416,448,480,0,32,64,96,128,160,192,224,256,288,320},{353,385,4..., dimensions={0} | all-to-all | bytes 524288 | tf_op jit(solution)/shard_map/prefix/all_to_all | solution.py:225
  39.3 0.0 copy-done.2
  39.3 0.0 copy-done.1
  39.3 0.0 copy-done
  39.3 0.0 copy-done.3
  39.3 0.0 copy-done.4
  39.3 1.4 %attended.1 = (f32[512,512]{1,0:T(8,128)S(1)}, bf16[4,3,256,256]{3,2,1,0:T(8,128)(2,1)S(1)}, f32[8,2,512]{2,1,0:T(2,128)S(1)}) custom-call(bf16[512,512]{1,0:T(8,128)(2,1)S(1)} %copy-done, bf16[512,512]{1,0:T(8,128)(2,1)S(1)} %copy-done.1, bf16[512,512]{1,0:T(8,128)(2,1)S(1)} %copy-done.2, f32[16,32,128]{2,1,0:T(8,128)S(1)} %all_to_all.26.refs_3_.refs_6_, ...), custom_call_target="tpu_custom_call" | custom-call | tf_op jit(solution)/shard_map/attended/pallas_call | solution.py:46
  40.7 10.8 %all_to_all.27.refs_0_ = f32[8,2,512]{2,1,0:T(2,128)S(1)} all-to-all(f32[8,2,512]{2,1,0:T(2,128)S(1)} %get-tuple-element.10), channel_id=1, replica_groups={{16,20,24,28,0,4,8,12},{17,21,25,29,1,5,9,13},{18,22,26,30,2,6,10,14},{..., dimensions={0} | all-to-all | bytes 65536 | tf_op jit(solution)/shard_map/attended/all_to_all | solution.py:225
  51.5 0.8 norm.1
  52.3 14.4 %all_to_all.28.part_ref = f32[16,32,128]{2,1,0:T(8,128)S(1)} all-to-all(f32[16,32,128]{2,1,0:T(8,128)S(1)} %get-tuple-element.12), channel_id=1, replica_groups={{352,384,416,448,480,0,32,64,96,128,160,192,224,256,288,320},{353,385,4..., dimensions={0} | all-to-all | bytes 524288 | tf_op jit(solution)/shard_map/suffix/all_to_all | solution.py:225
  66.7 14.2 %all_to_all.29.refs_0_ = f32[16,32,128]{2,1,0:T(8,128)S(1)} all-to-all(f32[16,32,128]{2,1,0:T(8,128)S(1)} %suffix.1), channel_id=1, replica_groups={{352,384,416,448,480,0,32,64,96,128,160,192,224,256,288,320},{353,385,4..., dimensions={0} | all-to-all | bytes 524288 | tf_op jit(solution)/shard_map/suffix/all_to_all | solution.py:225
  80.9 3.1 %grads.1 = (bf16[512,512]{1,0:T(8,128)(2,1)}, bf16[512,512]{1,0:T(8,128)(2,1)}, bf16[512,512]{1,0:T(8,128)(2,1)}, bf16[512,512]{1,0:T(8,128)(2,1)}) custom-call(f32[16,32,128]{2,1,0:T(8,128)S(1)} %all_to_all.29.refs_0_, bf16[512,512]{1,0:T(8,128)(2,1)S(1)} %get-tuple-element.13.refs_1_, bf16[512,512]{1,0:T(8,128)(2,1)S(1)} %copy-done, ...), custom_call_target="tpu_custom_call" | custom-call | tf_op jit(solution)/shard_map/grads/pallas_call | solution.py:46
  (2 shorter events, 0.0 us)
Async XLA Ops:
  0.6 38.7 %copy-start.2 = (bf16[512,512]{1,0:T(8,128)(2,1)S(1)}, bf16[512,512]{1,0:T(8,128)(2,1)}, u32[]{:S(2)}) copy-start(bf16[512,512]{1,0:T(8,128)(2,1)} %refs_4_.5) | copy-start | bytes 1572868
  0.6 38.7 %copy-start.1 = (bf16[512,512]{1,0:T(8,128)(2,1)S(1)}, bf16[512,512]{1,0:T(8,128)(2,1)}, u32[]{:S(2)}) copy-start(bf16[512,512]{1,0:T(8,128)(2,1)} %refs_3_.1) | copy-start | bytes 1572868
  0.7 38.7 %copy-start = (bf16[512,512]{1,0:T(8,128)(2,1)S(1)}, bf16[512,512]{1,0:T(8,128)(2,1)}, u32[]{:S(2)}) copy-start(bf16[512,512]{1,0:T(8,128)(2,1)} %refs_2_.5) | copy-start | bytes 1572868
  0.7 38.7 %copy-start.3 = (bf16[512,512]{1,0:T(8,128)(2,1)S(1)}, bf16[512,512]{1,0:T(8,128)(2,1)}, u32[]{:S(2)}) copy-start(bf16[512,512]{1,0:T(8,128)(2,1)} %refs_2_.4) | copy-start | bytes 1572868
  0.7 38.7 %copy-start.4 = (f32[512]{0:T(512)S(1)}, f32[512]{0:T(512)}, u32[]{:S(2)}) copy-start(f32[512]{0:T(512)} %param.8) | copy-start | bytes 6148

commit v5 on v4

--- a/solution.py
+++ b/solution.py
@@ -12,8 +12,8 @@
 EPS = 1e-06
 F32 = jnp.float32
 BF16 = jnp.bfloat16
-FORWARD_FIRST = 11
-BACKWARD_FIRST = 11
+FORWARD_FIRST = 15
+BACKWARD_FIRST = 10
 HEAD_FIRST = 4
 VMEM_LIMIT = 24 * 1024 * 1024
 

time: 84.3 us -> 83.5 us (level)
  no operation moved by 1% of the time
where the time goes in v5:
time: 83.5 us; the launch traced here: 83.2 us
  blocking collectives  75.4 us (90%)
  Pallas kernels  7.03 us (8%)
    all_to_all x5, blocking collectives, exchange(): lax.all_to_all(parts, axis, 0, 0, tiled=True, axis_index_groups=[order])  75.4 us
    pallas_call x6, Pallas kernels, call(): pl.pallas_call(kernel, out_shape=out_shape, compiler_params=pltpu.Compile...  7.03 us

profile of v5, /device:TPU:64, one launch (start us, length us, event | category | flops | bytes accessed | tf_op | source)
XLA Modules:
  0.0 83.2 jit_solution(5674876146873934538)
XLA Ops:
  0.6 0.0 copy-start.2
  0.6 0.0 copy-start.1
  0.7 0.0 copy-start
  0.7 0.0 copy-start.3
  0.7 0.0 copy-start.4
  0.7 1.7 %key_value_state.1 = f32[16,32,128]{2,1,0:T(8,128)S(1)} custom-call(bf16[512,512]{1,0:T(8,128)(2,1)} %refs_3_.1, bf16[512,512]{1,0:T(8,128)(2,1)} %refs_4_.5), custom_call_target="tpu_custom_call" | custom-call | tf_op jit(solution)/shard_map/key_value_state/pallas_call | solution.py:46
  2.4 20.8 %all_to_all.25.part_ref = f32[16,32,128]{2,1,0:T(8,128)S(1)} all-to-all(f32[16,32,128]{2,1,0:T(8,128)S(1)} %key_value_state.1), channel_id=1, replica_groups={{480,0,32,64,96,128,160,192,224,256,288,320,352,384,416,448},{481,1,33,..., dimensions={0} | all-to-all | bytes 524288 | tf_op jit(solution)/shard_map/prefix/all_to_all | solution.py:225
  23.3 15.7 %all_to_all.26.refs_3_.refs_6_ = f32[16,32,128]{2,1,0:T(8,128)S(1)} all-to-all(f32[16,32,128]{2,1,0:T(8,128)S(1)} %prefix.1), channel_id=1, replica_groups={{480,0,32,64,96,128,160,192,224,256,288,320,352,384,416,448},{481,1,33,..., dimensions={0} | all-to-all | bytes 524288 | tf_op jit(solution)/shard_map/prefix/all_to_all | solution.py:225
  39.0 0.0 copy-done.2
  39.0 0.0 copy-done.1
  39.0 0.0 copy-done
  39.0 0.0 copy-done.3
  39.0 0.0 copy-done.4
  39.0 1.4 %attended.1 = (f32[512,512]{1,0:T(8,128)S(1)}, bf16[4,3,256,256]{3,2,1,0:T(8,128)(2,1)S(1)}, f32[8,2,512]{2,1,0:T(2,128)S(1)}) custom-call(bf16[512,512]{1,0:T(8,128)(2,1)S(1)} %copy-done, bf16[512,512]{1,0:T(8,128)(2,1)S(1)} %copy-done.1, bf16[512,512]{1,0:T(8,128)(2,1)S(1)} %copy-done.2, f32[16,32,128]{2,1,0:T(8,128)S(1)} %all_to_all.26.refs_3_.refs_6_, ...), custom_call_target="tpu_custom_call" | custom-call | tf_op jit(solution)/shard_map/attended/pallas_call | solution.py:46
  40.4 10.8 %all_to_all.27.refs_0_ = f32[8,2,512]{2,1,0:T(2,128)S(1)} all-to-all(f32[8,2,512]{2,1,0:T(2,128)S(1)} %get-tuple-element.10), channel_id=1, replica_groups={{16,20,24,28,0,4,8,12},{17,21,25,29,1,5,9,13},{18,22,26,30,2,6,10,14},{..., dimensions={0} | all-to-all | bytes 65536 | tf_op jit(solution)/shard_map/attended/all_to_all | solution.py:225
  51.2 0.8 norm.1
  52.0 13.9 %all_to_all.28.part_ref = f32[16,32,128]{2,1,0:T(8,128)S(1)} all-to-all(f32[16,32,128]{2,1,0:T(8,128)S(1)} %get-tuple-element.12), channel_id=1, replica_groups={{320,352,384,416,448,480,0,32,64,96,128,160,192,224,256,288},{321,353,3..., dimensions={0} | all-to-all | bytes 524288 | tf_op jit(solution)/shard_map/suffix/all_to_all | solution.py:225
  65.9 14.2 %all_to_all.29.refs_0_ = f32[16,32,128]{2,1,0:T(8,128)S(1)} all-to-all(f32[16,32,128]{2,1,0:T(8,128)S(1)} %suffix.1), channel_id=1, replica_groups={{320,352,384,416,448,480,0,32,64,96,128,160,192,224,256,288},{321,353,3..., dimensions={0} | all-to-all | bytes 524288 | tf_op jit(solution)/shard_map/suffix/all_to_all | solution.py:225
  80.1 3.1 %grads.1 = (bf16[512,512]{1,0:T(8,128)(2,1)}, bf16[512,512]{1,0:T(8,128)(2,1)}, bf16[512,512]{1,0:T(8,128)(2,1)}, bf16[512,512]{1,0:T(8,128)(2,1)}) custom-call(f32[16,32,128]{2,1,0:T(8,128)S(1)} %all_to_all.29.refs_0_, bf16[512,512]{1,0:T(8,128)(2,1)S(1)} %get-tuple-element.13.refs_1_, bf16[512,512]{1,0:T(8,128)(2,1)S(1)} %copy-done, ...), custom_call_target="tpu_custom_call" | custom-call | tf_op jit(solution)/shard_map/grads/pallas_call | solution.py:46
  (2 shorter events, 0.0 us)
Async XLA Ops:
  0.6 38.4 %copy-start.2 = (bf16[512,512]{1,0:T(8,128)(2,1)S(1)}, bf16[512,512]{1,0:T(8,128)(2,1)}, u32[]{:S(2)}) copy-start(bf16[512,512]{1,0:T(8,128)(2,1)} %refs_4_.5) | copy-start | bytes 1572868
  0.6 38.4 %copy-start.1 = (bf16[512,512]{1,0:T(8,128)(2,1)S(1)}, bf16[512,512]{1,0:T(8,128)(2,1)}, u32[]{:S(2)}) copy-start(bf16[512,512]{1,0:T(8,128)(2,1)} %refs_3_.1) | copy-start | bytes 1572868
  0.7 38.4 %copy-start = (bf16[512,512]{1,0:T(8,128)(2,1)S(1)}, bf16[512,512]{1,0:T(8,128)(2,1)}, u32[]{:S(2)}) copy-start(bf16[512,512]{1,0:T(8,128)(2,1)} %refs_2_.5) | copy-start | bytes 1572868
  0.7 38.4 %copy-start.3 = (bf16[512,512]{1,0:T(8,128)(2,1)S(1)}, bf16[512,512]{1,0:T(8,128)(2,1)}, u32[]{:S(2)}) copy-start(bf16[512,512]{1,0:T(8,128)(2,1)} %refs_2_.4) | copy-start | bytes 1572868
  0.7 38.4 %copy-start.4 = (f32[512]{0:T(512)S(1)}, f32[512]{0:T(512)}, u32[]{:S(2)}) copy-start(f32[512]{0:T(512)} %param.8) | copy-start | bytes 6148

commit v6 on v5

--- a/solution.py
+++ b/solution.py
@@ -12,8 +12,8 @@
 EPS = 1e-06
 F32 = jnp.float32
 BF16 = jnp.bfloat16
-FORWARD_FIRST = 15
-BACKWARD_FIRST = 10
+FORWARD_FIRST = (15, 11)
+BACKWARD_FIRST = (10, 10)
 HEAD_FIRST = 4
 VMEM_LIMIT = 24 * 1024 * 1024
 
@@ -55,8 +55,9 @@
     return jax.ShapeDtypeStruct(shape, dtype)
 
 
-def state_of_heads(ref, heads):
-    return ref[...].reshape(heads, HD, HD).astype(BF16)
+def state_of_heads(ref, slots, heads):
+    chunks = jnp.concatenate([ref[slot] for slot in slots], axis=0)
+    return chunks.reshape(heads, HD, HD).astype(BF16)
 
 
 def store_state(state_ref, heads, h, state):
@@ -86,12 +87,12 @@
         store_state(state_ref, heads, h, states[h])
 
 
-def scan_kernel(slots, part_ref, out_ref):
+def scan_kernel(devices, there, back, part_ref, out_ref):
     total = jnp.zeros(part_ref.shape[1:], F32)
-    for slot in slots:
-        out_ref[slot] = total
-        if slot != slots[-1]:
-            total = total + part_ref[slot]
+    for device in devices:
+        out_ref[back.index(device)] = total
+        if device != devices[-1]:
+            total = total + part_ref[there.index(device)]
 
 
 def causal_mask(rows):
@@ -108,9 +109,9 @@
     return slice(0, tokens // 2), slice(tokens // 2, tokens)
 
 
-def attend_kernel(heads, q_ref, k_ref, v_ref, p_ref, c_ref, g_ref, a_ref, w_ref, sums_ref):
+def attend_kernel(prefix_slots, heads, q_ref, k_ref, v_ref, p_ref, c_ref, g_ref, a_ref, w_ref, sums_ref):
     tokens = q_ref.shape[0]
-    state = state_of_heads(p_ref, heads)
+    state = state_of_heads(p_ref, prefix_slots, heads)
     mask = causal_mask(tokens // 2)
     first, second = halves(tokens)
     squares = [jnp.zeros((tokens // 2, HD), F32)] * 2
@@ -136,13 +137,9 @@
         )
         for i, rows in enumerate((first, second)):
             a_ref[rows, cols] = attended[i]
-    for h in range(heads):
-        cols = head_columns(h)
-        for i, rows in enumerate((first, second)):
-            part = a_ref[rows, cols]
             scaled = c_ref[rows, cols].astype(F32) * g_ref[:, cols]
-            squares[i] = squares[i] + part * part
-            inner[i] = inner[i] + scaled * part
+            squares[i] = squares[i] + attended[i] * attended[i]
+            inner[i] = inner[i] + scaled * attended[i]
     squares = jnp.concatenate([jnp.sum(part.T, axis=0, keepdims=True) for part in squares], axis=1)
     inner = jnp.concatenate([jnp.sum(part.T, axis=0, keepdims=True) for part in inner], axis=1)
     both = jnp.concatenate([squares, inner], axis=0)
@@ -175,7 +172,7 @@
 
 
 def grad_kernel(
-    heads, r_ref, d_ref, q_ref, k_ref, v_ref, w_ref, p_ref, o_ref,
+    prefix_slots, suffix_slots, heads, r_ref, d_ref, q_ref, k_ref, v_ref, w_ref, p_ref, o_ref,
     o_hbm, gq_hbm, gk_hbm, gv_hbm, gq_ref, gk_ref, gv_ref, gw_ref, sems,
 ):
     copies = []
@@ -191,8 +188,8 @@
     tokens = q_ref.shape[0]
     first, second = halves(tokens)
     mask = causal_mask(tokens // 2)
-    prefix = state_of_heads(p_ref, heads)
-    suffix = state_of_heads(r_ref, heads)
+    prefix = state_of_heads(p_ref, prefix_slots, heads)
+    suffix = state_of_heads(r_ref, suffix_slots, heads)
     for h in range(heads):
         cols = head_columns(h)
         v0, v1 = v_ref[first, cols], v_ref[second, cols]
@@ -225,10 +222,11 @@
     return lax.all_to_all(parts, axis, 0, 0, tiled=True, axis_index_groups=[order])
 
 
-def exclusive_scan(local, slots, order):
-    pieces = exchange(local, "seq", order)
-    sums = call(functools.partial(scan_kernel, slots), shape_of(local.shape), pieces)
-    return exchange(sums, "seq", order)
+def exclusive_scan(local, devices, there, back):
+    pieces = exchange(local, "seq", there)
+    kernel = functools.partial(scan_kernel, devices, there, back)
+    sums = call(kernel, shape_of(local.shape), pieces)
+    return exchange(sums, "seq", back), [back.index(device) for device in there]
 
 
 def per_device(queries, key_vectors, value_vectors, norm_gain, cotangent):
@@ -261,11 +259,11 @@
             ],
         )
     with jax.named_scope("prefix"):
-        order = rotated(seq, FORWARD_FIRST)
-        prefix = exclusive_scan(local_kv, [order.index(m) for m in range(seq)], order)
+        there, back = (rotated(seq, first) for first in FORWARD_FIRST)
+        prefix, prefix_slots = exclusive_scan(local_kv, list(range(seq)), there, back)
     with jax.named_scope("attended"):
         attended, weights, sums = call(
-            bind(attend_kernel),
+            bind(functools.partial(attend_kernel, prefix_slots)),
             (
                 shape_of(wide),
                 shape_of((heads, 3, tokens // 2, tokens // 2), BF16),
@@ -290,11 +288,11 @@
             queries,
         )
     with jax.named_scope("suffix"):
-        order = rotated(seq, BACKWARD_FIRST)
-        suffix = exclusive_scan(local_qg, [order.index(m) for m in reversed(range(seq))], order)
+        there, back = (rotated(seq, first) for first in BACKWARD_FIRST)
+        suffix, suffix_slots = exclusive_scan(local_qg, list(range(seq))[::-1], there, back)
     with jax.named_scope("grads"):
         return call(
-            bind(grad_kernel),
+            bind(functools.partial(grad_kernel, prefix_slots, suffix_slots)),
             (shape_of(wide, BF16),) * 4,
             suffix,
             out_grad,

time: 83.5 us -> 83.3 us (level)
  no operation moved by 1% of the time
where the time goes in v6:
time: 83.3 us; the launch traced here: 83 us
  blocking collectives  75.2 us (90%)
  Pallas kernels  6.97 us (8%)
    all_to_all x5, blocking collectives, exchange(): lax.all_to_all(parts, axis, 0, 0, tiled=True, axis_index_groups=[order])  75.2 us
    pallas_call x6, Pallas kernels, call(): pl.pallas_call(kernel, out_shape=out_shape, compiler_params=pltpu.Compile...  6.97 us

profile of v6, /device:TPU:64, one launch (start us, length us, event | category | flops | bytes accessed | tf_op | source)
XLA Modules:
  0.0 83.0 jit_solution(3017290619937655910)
XLA Ops:
  0.6 0.0 copy-start.2
  0.6 0.0 copy-start.1
  0.7 0.0 copy-start
  0.7 0.0 copy-start.3
  0.7 0.0 copy-start.4
  0.7 1.7 %key_value_state.1 = f32[16,32,128]{2,1,0:T(8,128)S(1)} custom-call(bf16[512,512]{1,0:T(8,128)(2,1)} %refs_3_.1, bf16[512,512]{1,0:T(8,128)(2,1)} %refs_4_.5), custom_call_target="tpu_custom_call" | custom-call | tf_op jit(solution)/shard_map/key_value_state/pallas_call | solution.py:46
  2.4 20.8 %all_to_all.25.part_ref = f32[16,32,128]{2,1,0:T(8,128)S(1)} all-to-all(f32[16,32,128]{2,1,0:T(8,128)S(1)} %key_value_state.1), channel_id=1, replica_groups={{480,0,32,64,96,128,160,192,224,256,288,320,352,384,416,448},{481,1,33,..., dimensions={0} | all-to-all | bytes 524288 | tf_op jit(solution)/shard_map/prefix/all_to_all | solution.py:222
  23.3 15.7 %all_to_all.26.refs_3_.refs_6_ = f32[16,32,128]{2,1,0:T(8,128)S(1)} all-to-all(f32[16,32,128]{2,1,0:T(8,128)S(1)} %prefix.1), channel_id=1, replica_groups={{352,384,416,448,480,0,32,64,96,128,160,192,224,256,288,320},{353,385,4..., dimensions={0} | all-to-all | bytes 524288 | tf_op jit(solution)/shard_map/prefix/all_to_all | solution.py:222
  39.0 0.0 copy-done.2
  39.0 0.0 copy-done.1
  39.0 0.0 copy-done
  39.0 0.0 copy-done.3
  39.0 0.0 copy-done.4
  39.0 1.3 %attended.1 = (f32[512,512]{1,0:T(8,128)S(1)}, bf16[4,3,256,256]{3,2,1,0:T(8,128)(2,1)S(1)}, f32[8,2,512]{2,1,0:T(2,128)S(1)}) custom-call(bf16[512,512]{1,0:T(8,128)(2,1)S(1)} %copy-done, bf16[512,512]{1,0:T(8,128)(2,1)S(1)} %copy-done.1, bf16[512,512]{1,0:T(8,128)(2,1)S(1)} %copy-done.2, f32[16,32,128]{2,1,0:T(8,128)S(1)} %all_to_all.26.refs_3_.refs_6_, ...), custom_call_target="tpu_custom_call" | custom-call | tf_op jit(solution)/shard_map/attended/pallas_call | solution.py:46
  40.4 10.8 %all_to_all.27.refs_0_ = f32[8,2,512]{2,1,0:T(2,128)S(1)} all-to-all(f32[8,2,512]{2,1,0:T(2,128)S(1)} %get-tuple-element.10), channel_id=1, replica_groups={{16,20,24,28,0,4,8,12},{17,21,25,29,1,5,9,13},{18,22,26,30,2,6,10,14},{..., dimensions={0} | all-to-all | bytes 65536 | tf_op jit(solution)/shard_map/attended/all_to_all | solution.py:222
  51.2 0.8 norm.1
  51.9 13.8 %all_to_all.28.part_ref = f32[16,32,128]{2,1,0:T(8,128)S(1)} all-to-all(f32[16,32,128]{2,1,0:T(8,128)S(1)} %get-tuple-element.12), channel_id=1, replica_groups={{320,352,384,416,448,480,0,32,64,96,128,160,192,224,256,288},{321,353,3..., dimensions={0} | all-to-all | bytes 524288 | tf_op jit(solution)/shard_map/suffix/all_to_all | solution.py:222
  65.8 14.1 %all_to_all.29.refs_0_ = f32[16,32,128]{2,1,0:T(8,128)S(1)} all-to-all(f32[16,32,128]{2,1,0:T(8,128)S(1)} %suffix.1), channel_id=1, replica_groups={{320,352,384,416,448,480,0,32,64,96,128,160,192,224,256,288},{321,353,3..., dimensions={0} | all-to-all | bytes 524288 | tf_op jit(solution)/shard_map/suffix/all_to_all | solution.py:222
  79.9 3.1 %grads.1 = (bf16[512,512]{1,0:T(8,128)(2,1)}, bf16[512,512]{1,0:T(8,128)(2,1)}, bf16[512,512]{1,0:T(8,128)(2,1)}, bf16[512,512]{1,0:T(8,128)(2,1)}) custom-call(f32[16,32,128]{2,1,0:T(8,128)S(1)} %all_to_all.29.refs_0_, bf16[512,512]{1,0:T(8,128)(2,1)S(1)} %get-tuple-element.13.refs_1_, bf16[512,512]{1,0:T(8,128)(2,1)S(1)} %copy-done, ...), custom_call_target="tpu_custom_call" | custom-call | tf_op jit(solution)/shard_map/grads/pallas_call | solution.py:46
  (2 shorter events, 0.0 us)
Async XLA Ops:
  0.6 38.4 %copy-start.2 = (bf16[512,512]{1,0:T(8,128)(2,1)S(1)}, bf16[512,512]{1,0:T(8,128)(2,1)}, u32[]{:S(2)}) copy-start(bf16[512,512]{1,0:T(8,128)(2,1)} %refs_4_.5) | copy-start | bytes 1572868
  0.6 38.4 %copy-start.1 = (bf16[512,512]{1,0:T(8,128)(2,1)S(1)}, bf16[512,512]{1,0:T(8,128)(2,1)}, u32[]{:S(2)}) copy-start(bf16[512,512]{1,0:T(8,128)(2,1)} %refs_3_.1) | copy-start | bytes 1572868
  0.7 38.4 %copy-start = (bf16[512,512]{1,0:T(8,128)(2,1)S(1)}, bf16[512,512]{1,0:T(8,128)(2,1)}, u32[]{:S(2)}) copy-start(bf16[512,512]{1,0:T(8,128)(2,1)} %refs_2_.5) | copy-start | bytes 1572868
  0.7 38.4 %copy-start.3 = (bf16[512,512]{1,0:T(8,128)(2,1)S(1)}, bf16[512,512]{1,0:T(8,128)(2,1)}, u32[]{:S(2)}) copy-start(bf16[512,512]{1,0:T(8,128)(2,1)} %refs_2_.4) | copy-start | bytes 1572868
  0.7 38.4 %copy-start.4 = (f32[512]{0:T(512)S(1)}, f32[512]{0:T(512)}, u32[]{:S(2)}) copy-start(f32[512]{0:T(512)} %param.8) | copy-start | bytes 6148

commit v7 on v6

--- a/solution.py
+++ b/solution.py
@@ -14,7 +14,7 @@
 BF16 = jnp.bfloat16
 FORWARD_FIRST = (15, 11)
 BACKWARD_FIRST = (10, 10)
-HEAD_FIRST = 4
+HEAD_FIRST = 5
 VMEM_LIMIT = 24 * 1024 * 1024
 
 
@@ -109,7 +109,7 @@
     return slice(0, tokens // 2), slice(tokens // 2, tokens)
 
 
-def attend_kernel(prefix_slots, heads, q_ref, k_ref, v_ref, p_ref, c_ref, g_ref, a_ref, w_ref, sums_ref):
+def attend_kernel(prefix_slots, heads, q_ref, k_ref, v_ref, p_ref, c_ref, g_ref, a_ref, wt_ref, sums_ref, w_ref):
     tokens = q_ref.shape[0]
     state = state_of_heads(p_ref, prefix_slots, heads)
     mask = causal_mask(tokens // 2)
@@ -126,6 +126,9 @@
         w_ref[h, 0] = w00
         w_ref[h, 1] = w10
         w_ref[h, 2] = w11
+        wt_ref[h, 0] = w00.T
+        wt_ref[h, 1] = w10.T
+        wt_ref[h, 2] = w11.T
     for h in range(heads):
         cols = head_columns(h)
         q0, q1 = q_ref[first, cols], q_ref[second, cols]
@@ -211,8 +214,8 @@
         gk_ref[second, cols] = (nt(v1, suffix[h]) + tn(g11, q1)).astype(BF16)
         send(2, h, gk_ref, gk_hbm)
         w00, w10, w11 = w_ref[h, 0], w_ref[h, 1], w_ref[h, 2]
-        gv_ref[first, cols] = (nn(k0, suffix[h]) + (tn(w00, d0) + tn(w10, d1))).astype(BF16)
-        gv_ref[second, cols] = (nn(k1, suffix[h]) + tn(w11, d1)).astype(BF16)
+        gv_ref[first, cols] = (nn(k0, suffix[h]) + (nn(w00, d0) + nn(w10, d1))).astype(BF16)
+        gv_ref[second, cols] = (nn(k1, suffix[h]) + nn(w11, d1)).astype(BF16)
         send(3, h, gv_ref, gv_hbm)
     for copy in copies:
         copy.wait()
@@ -275,6 +278,7 @@
             prefix,
             cotangent,
             gain,
+            scratch_shapes=[pltpu.VMEM((heads, 3, tokens // 2, tokens // 2), BF16)],
         )
         sums = exchange(sums, "head", rotated(head_devices, HEAD_FIRST))
     with jax.named_scope("norm"):

time: 83.3 us -> 83.4 us (level)
  no operation moved by 1% of the time
where the time goes in v7:
time: 83.4 us; the launch traced here: 83.1 us
  blocking collectives  75.4 us (90%)
  Pallas kernels  6.96 us (8%)
    all_to_all x5, blocking collectives, exchange(): lax.all_to_all(parts, axis, 0, 0, tiled=True, axis_index_groups=[order])  75.4 us
    pallas_call x6, Pallas kernels, call(): pl.pallas_call(kernel, out_shape=out_shape, compiler_params=pltpu.Compile...  6.96 us

profile of v7, /device:TPU:64, one launch (start us, length us, event | category | flops | bytes accessed | tf_op | source)
XLA Modules:
  0.0 83.1 jit_solution(6026952969287008683)
XLA Ops:
  0.6 0.0 copy-start.2
  0.6 0.0 copy-start.1
  0.7 0.0 copy-start
  0.7 0.0 copy-start.3
  0.7 0.0 copy-start.4
  0.7 1.7 %key_value_state.1 = f32[16,32,128]{2,1,0:T(8,128)S(1)} custom-call(bf16[512,512]{1,0:T(8,128)(2,1)} %refs_3_.1, bf16[512,512]{1,0:T(8,128)(2,1)} %refs_4_.5), custom_call_target="tpu_custom_call" | custom-call | tf_op jit(solution)/shard_map/key_value_state/pallas_call | solution.py:46
  2.4 20.8 %all_to_all.25.part_ref = f32[16,32,128]{2,1,0:T(8,128)S(1)} all-to-all(f32[16,32,128]{2,1,0:T(8,128)S(1)} %key_value_state.1), channel_id=1, replica_groups={{480,0,32,64,96,128,160,192,224,256,288,320,352,384,416,448},{481,1,33,..., dimensions={0} | all-to-all | bytes 524288 | tf_op jit(solution)/shard_map/prefix/all_to_all | solution.py:225
  23.3 15.7 %all_to_all.26.refs_3_.refs_6_ = f32[16,32,128]{2,1,0:T(8,128)S(1)} all-to-all(f32[16,32,128]{2,1,0:T(8,128)S(1)} %prefix.1), channel_id=1, replica_groups={{352,384,416,448,480,0,32,64,96,128,160,192,224,256,288,320},{353,385,4..., dimensions={0} | all-to-all | bytes 524288 | tf_op jit(solution)/shard_map/prefix/all_to_all | solution.py:225
  39.0 0.0 copy-done.2
  39.0 0.0 copy-done.1
  39.0 0.0 copy-done
  39.0 0.0 copy-done.3
  39.0 0.0 copy-done.4
  39.0 1.3 %attended.1 = (f32[512,512]{1,0:T(8,128)S(1)}, bf16[4,3,256,256]{3,2,1,0:T(8,128)(2,1)S(1)}, f32[8,2,512]{2,1,0:T(2,128)S(1)}) custom-call(bf16[512,512]{1,0:T(8,128)(2,1)S(1)} %copy-done, bf16[512,512]{1,0:T(8,128)(2,1)S(1)} %copy-done.1, bf16[512,512]{1,0:T(8,128)(2,1)S(1)} %copy-done.2, f32[16,32,128]{2,1,0:T(8,128)S(1)} %all_to_all.26.refs_3_.refs_6_, ...), custom_call_target="tpu_custom_call" | custom-call | tf_op jit(solution)/shard_map/attended/pallas_call | solution.py:46
  40.4 11.0 %all_to_all.27.refs_0_ = f32[8,2,512]{2,1,0:T(2,128)S(1)} all-to-all(f32[8,2,512]{2,1,0:T(2,128)S(1)} %get-tuple-element.10), channel_id=1, replica_groups={{20,24,28,0,4,8,12,16},{21,25,29,1,5,9,13,17},{22,26,30,2,6,10,14,18},{..., dimensions={0} | all-to-all | bytes 65536 | tf_op jit(solution)/shard_map/attended/all_to_all | solution.py:225
  51.4 0.8 norm.1
  52.1 13.8 %all_to_all.28.part_ref = f32[16,32,128]{2,1,0:T(8,128)S(1)} all-to-all(f32[16,32,128]{2,1,0:T(8,128)S(1)} %get-tuple-element.12), channel_id=1, replica_groups={{320,352,384,416,448,480,0,32,64,96,128,160,192,224,256,288},{321,353,3..., dimensions={0} | all-to-all | bytes 524288 | tf_op jit(solution)/shard_map/suffix/all_to_all | solution.py:225
  66.0 14.1 %all_to_all.29.refs_0_ = f32[16,32,128]{2,1,0:T(8,128)S(1)} all-to-all(f32[16,32,128]{2,1,0:T(8,128)S(1)} %suffix.1), channel_id=1, replica_groups={{320,352,384,416,448,480,0,32,64,96,128,160,192,224,256,288},{321,353,3..., dimensions={0} | all-to-all | bytes 524288 | tf_op jit(solution)/shard_map/suffix/all_to_all | solution.py:225
  80.1 3.0 %grads.1 = (bf16[512,512]{1,0:T(8,128)(2,1)}, bf16[512,512]{1,0:T(8,128)(2,1)}, bf16[512,512]{1,0:T(8,128)(2,1)}, bf16[512,512]{1,0:T(8,128)(2,1)}) custom-call(f32[16,32,128]{2,1,0:T(8,128)S(1)} %all_to_all.29.refs_0_, bf16[512,512]{1,0:T(8,128)(2,1)S(1)} %get-tuple-element.13.refs_1_, bf16[512,512]{1,0:T(8,128)(2,1)S(1)} %copy-done, ...), custom_call_target="tpu_custom_call" | custom-call | tf_op jit(solution)/shard_map/grads/pallas_call | solution.py:46
  (2 shorter events, 0.0 us)
Async XLA Ops:
  0.6 38.4 %copy-start.2 = (bf16[512,512]{1,0:T(8,128)(2,1)S(1)}, bf16[512,512]{1,0:T(8,128)(2,1)}, u32[]{:S(2)}) copy-start(bf16[512,512]{1,0:T(8,128)(2,1)} %refs_4_.5) | copy-start | bytes 1572868
  0.6 38.4 %copy-start.1 = (bf16[512,512]{1,0:T(8,128)(2,1)S(1)}, bf16[512,512]{1,0:T(8,128)(2,1)}, u32[]{:S(2)}) copy-start(bf16[512,512]{1,0:T(8,128)(2,1)} %refs_3_.1) | copy-start | bytes 1572868
  0.7 38.4 %copy-start = (bf16[512,512]{1,0:T(8,128)(2,1)S(1)}, bf16[512,512]{1,0:T(8,128)(2,1)}, u32[]{:S(2)}) copy-start(bf16[512,512]{1,0:T(8,128)(2,1)} %refs_2_.5) | copy-start | bytes 1572868
  0.7 38.4 %copy-start.3 = (bf16[512,512]{1,0:T(8,128)(2,1)S(1)}, bf16[512,512]{1,0:T(8,128)(2,1)}, u32[]{:S(2)}) copy-start(bf16[512,512]{1,0:T(8,128)(2,1)} %refs_2_.4) | copy-start | bytes 1572868
  0.7 38.4 %copy-start.4 = (f32[512]{0:T(512)S(1)}, f32[512]{0:T(512)}, u32[]{:S(2)}) copy-start(f32[512]{0:T(512)} %param.8) | copy-start | bytes 6148
